TPU v7x, 32 devices: a whole 2x2x4 slice. The times are simulated.
32 devices in a mesh: gx: 2 (over y), gy: 16 (over z, x, core).
Axes of the slice: x: 2, y: 2, z: 4, core: 2. Of those that a mesh axis runs over, the one named last changes fastest.
Arguments:
- hidden_states_in: bfloat16 [32, 512, 768], P(('gx', 'gy')), may hold values from -6 to 6
- piece_sizes: int32 [32, 8], P(('gx', 'gy')), may hold values from 1 to 88, as said below
- matching_passage_number: int32 [128], P(('gx', 'gy')), may hold values from 0 to 127, each once
- softmax_sharpness: float32 [1], replicated, may hold values from 0.02 to 0.04
- question_projection: bfloat16 [768, 768], replicated, may hold values from -0.21875 to 0.21875
- question_offset: bfloat16 [768], replicated, may hold values from -2 to 2
- lookup_projection: bfloat16 [768, 768], replicated, may hold values from -0.21875 to 0.21875
- content_projection: bfloat16 [768, 768], replicated, may hold values from -0.21875 to 0.21875
- content_offset: bfloat16 [768], replicated, may hold values from -2 to 2
- mixing_result_projection: bfloat16 [768, 768], replicated, may hold values from -1.5 to 1.5
- mixing_result_offset: bfloat16 [768], replicated, may hold values from -2 to 2
- mixing_layernorm_scale: bfloat16 [768], replicated, may hold values from 0.5 to 1.5
- mixing_layernorm_offset: bfloat16 [768], replicated, may hold values from -2 to 2
- widening_projection: bfloat16 [768, 3072], replicated, may hold values from -0.21875 to 0.21875
- widening_offset: bfloat16 [3072], replicated, may hold values from -2 to 2
- narrowing_projection: bfloat16 [3072, 768], replicated, may hold values from -0.109375 to 0.109375
- narrowing_offset: bfloat16 [768], replicated, may hold values from -2 to 2
- perceptron_layernorm_scale: bfloat16 [768], replicated, may hold values from 0.5 to 1.5
- perceptron_layernorm_offset: bfloat16 [768], replicated, may hold values from -0.5 to 0.5
Outputs:
- loss: float32 [1], replicated
- pooled: float32 [32, 8, 768], P(('gx', 'gy'))
- grad_tokens: float32 [32, 512, 768], P(('gx', 'gy'))
- grad_w_query: float32 [768, 768], P('gy')
- grad_b_query: float32 [768], P('gy')
- grad_w_key: float32 [768, 768], P('gy')
- grad_w_value: float32 [768, 768], P('gy')
- grad_b_value: float32 [768], P('gy')
- grad_w_output: float32 [768, 768], P('gy')
- grad_b_output: float32 [768], P('gy')
- grad_gain_attn: float32 [768], P('gy')
- grad_shift_attn: float32 [768], P('gy')
- grad_w_inner: float32 [768, 3072], P('gy')
- grad_b_inner: float32 [3072], P('gy')
- grad_w_outer: float32 [3072, 768], P('gy')
- grad_b_outer: float32 [768], P('gy')
- grad_gain_ffn: float32 [768], P('gy')
- grad_shift_ffn: float32 [768], P('gy')
Inputs may be any that keep to these rules, and one draw needn't show every extreme that they name: `piece_sizes`: segments alternate query, document, beginning with a query; a query has at most 32 tokens, a document at least 32; segments fill each row from its start and the rest of the row is padding. `matching_passage_number`: every document is the positive of exactly one query.
All inputs are finite; a program needn't handle non-finite values.
Results may differ from a plain program's by a relative error of at most 0.015.
Values may be sent and summed in bfloat16 or wider, within the bound.
No kernel may reach another device: no remote copies, remote signals or barrier semaphores. Data moves between devices by JAX's collectives and lax.ppermute only.
A program may use at most 192 MiB of HBM per device.

v0:
```python
import jax
import jax.numpy as jnp
from jax import lax
from jax.sharding import PartitionSpec as P

HEADS = 12
HD = 64


EPS_NORM = 1e-12
EPS_UNIT = 1e-06
NEG_FILL = -1e30
FULL_ACCURACY = lax.Precision.HIGHEST


def membership(piece_sizes, length):
    seg_ends = jnp.cumsum(piece_sizes, axis=-1)
    seg_starts = seg_ends - piece_sizes
    places = jnp.arange(length, dtype=jnp.int32)
    return (places[None, None, :] >= seg_starts[:, :, None]) & (
        places[None, None, :] < seg_ends[:, :, None]
    )


def standardize(hidden):
    center = hidden - jnp.mean(hidden, axis=-1, keepdims=True)
    inv_scale = lax.rsqrt(jnp.mean(center * center, axis=-1, keepdims=True) + EPS_NORM)
    return (center * inv_scale, inv_scale)


def standardize_back(normed, inv_scale, grad_normed):
    mean_grad = jnp.mean(grad_normed, axis=-1, keepdims=True)
    mean_both = jnp.mean(grad_normed * normed, axis=-1, keepdims=True)
    return inv_scale * (grad_normed - mean_grad - normed * mean_both)


def gelu_slope(values):
    normal_cdf = 0.5 * (1.0 + lax.erf(values * 0.7071067811865476))
    normal_pdf = jnp.exp(-0.5 * values * values) * 0.3989422804014327
    return normal_cdf + values * normal_pdf


def contract_rows(left, right):
    return lax.dot_general(
        left, right, (((0,), (0,)), ((), ())), preferred_element_type=jnp.float32
    )


def reduce_along_second_axis(left, right):
    return lax.dot_general(
        left, right, (((1,), (1,)), ((), ())), preferred_element_type=jnp.float32
    )


def row_scores(row_query, row_keys, row_seg):
    allowed = row_seg[:, None] == row_seg[None, :]
    scores = jnp.einsum(
        "qhd,khd->hqk", row_query, row_keys, preferred_element_type=jnp.float32
    ) * HD ** (-0.5)
    return jnp.where(allowed[None], scores, NEG_FILL)


def attend_row(element):
    row_query, row_keys, row_values, row_seg = element
    scores = row_scores(row_query, row_keys, row_seg)
    top_score = jnp.max(scores, axis=-1, keepdims=True)
    expo = jnp.exp(scores - top_score)
    total = jnp.sum(expo, axis=-1, keepdims=True)
    probs_low = (expo / total).astype(jnp.bfloat16)
    mixed = jnp.einsum("hqk,khd->qhd", probs_low, row_values, preferred_element_type=jnp.float32)
    return (mixed.astype(jnp.bfloat16), (top_score + jnp.log(total))[..., 0])


def attend_back(element):
    row_query, row_keys, row_values, row_seg, row_lse, row_grad = element
    scores = row_scores(row_query, row_keys, row_seg)
    probs = jnp.exp(scores - row_lse[..., None])
    probs_low = probs.astype(jnp.bfloat16)
    grad_values = jnp.einsum(
        "hqk,qhd->khd", probs_low, row_grad, preferred_element_type=jnp.float32
    )
    grad_probs = jnp.einsum(
        "qhd,khd->hqk", row_grad, row_values, preferred_element_type=jnp.float32
    )
    inner = jnp.sum(grad_probs * probs, axis=-1, keepdims=True)
    grad_scores = (probs * (grad_probs - inner)).astype(jnp.bfloat16)
    grad_query = jnp.einsum(
        "hqk,khd->qhd", grad_scores, row_keys, preferred_element_type=jnp.float32
    ) * HD ** (-0.5)
    grad_keys = jnp.einsum(
        "hqk,qhd->khd", grad_scores, row_query, preferred_element_type=jnp.float32
    ) * HD ** (-0.5)
    return (
        grad_query.astype(jnp.bfloat16),
        grad_keys.astype(jnp.bfloat16),
        grad_values.astype(jnp.bfloat16),
    )


def arrange(packed, groups_y, groups_x):
    block = packed.shape[0] // groups_y
    sub = -(-block // groups_x)
    columns = packed.shape[1]
    view = packed.reshape(groups_y, block, columns)
    view = jnp.swapaxes(view.reshape(groups_y, groups_x, sub, columns), 0, 1)
    return view.reshape(groups_x * groups_y * sub, columns)


def reduce_main(packed, local_loss):
    groups_y = lax.axis_size("gy")
    groups_x = lax.axis_size("gx")
    loss_terms = jnp.full((groups_x * groups_y,), local_loss, jnp.float32)
    share, loss_share = (
        lax.psum_scatter(
            arrange(packed, groups_y, groups_x), ("gx", "gy"), scatter_dimension=0, tiled=True
        ),
        lax.psum_scatter(loss_terms, ("gx", "gy"), scatter_dimension=0, tiled=True),
    )
    whole = lax.all_gather(share.astype(jnp.bfloat16), "gx", axis=0, tiled=True).astype(share.dtype)
    return (whole, loss_share[0])


def pack(entries, width):
    return jnp.concatenate([entry.reshape(width, -1) for entry in entries], axis=1)


def unpack(share, entries, width):
    results = []
    offset = 0
    for entry in entries:
        columns = entry.size // width
        piece = share[:, offset : offset + columns]
        results.append(piece.reshape((-1,) + entry.shape[1:]))
        offset = offset + columns
    return results


def body(
    hidden_states_in,
    piece_sizes,
    matching_passage_number,
    softmax_sharpness,
    question_projection,
    question_offset,
    lookup_projection,
    content_projection,
    content_offset,
    mixing_result_projection,
    mixing_result_offset,
    mixing_layernorm_scale,
    mixing_layernorm_offset,
    widening_projection,
    widening_offset,
    narrowing_projection,
    narrowing_offset,
    perceptron_layernorm_scale,
    perceptron_layernorm_offset,
):
    rows_here, length, width = hidden_states_in.shape
    count_tokens = rows_here * length
    segments = piece_sizes.shape[1]
    half = segments // 2
    flat_tokens = hidden_states_in.reshape(count_tokens, width)
    member = membership(piece_sizes, length)
    numbers = jnp.arange(1, segments + 1, dtype=jnp.int32)
    token_seg = jnp.sum(member.astype(jnp.int32) * numbers[None, :, None], axis=1) - 1
    queries = (
        jnp.dot(flat_tokens, question_projection, preferred_element_type=jnp.float32)
        + question_offset
    ).astype(jnp.bfloat16)
    keys_proj = jnp.dot(flat_tokens, lookup_projection, preferred_element_type=jnp.float32).astype(
        jnp.bfloat16
    )
    values = (
        jnp.dot(flat_tokens, content_projection, preferred_element_type=jnp.float32)
        + content_offset
    ).astype(jnp.bfloat16)
    head_shape = (rows_here, length, HEADS, HD)
    query_rows = queries.reshape(head_shape)
    key_rows = keys_proj.reshape(head_shape)
    value_rows = values.reshape(head_shape)
    attn_rows, lse_rows = lax.map(attend_row, (query_rows, key_rows, value_rows, token_seg))
    attn_flat = attn_rows.reshape(count_tokens, width)
    hidden_one = (
        flat_tokens.astype(jnp.float32)
        + jnp.dot(attn_flat, mixing_result_projection, preferred_element_type=jnp.float32)
        + mixing_result_offset
    )
    normed_one, inv_one = standardize(hidden_one)
    out_one = normed_one * mixing_layernorm_scale + mixing_layernorm_offset
    out_one_low = out_one.astype(jnp.bfloat16)
    inner_pre = (
        jnp.dot(out_one_low, widening_projection, preferred_element_type=jnp.float32)
        + widening_offset
    )
    inner_low = jax.nn.gelu(inner_pre, approximate=False).astype(jnp.bfloat16)
    hidden_two = (
        out_one
        + jnp.dot(inner_low, narrowing_projection, preferred_element_type=jnp.float32)
        + narrowing_offset
    )
    normed_two, inv_two = standardize(hidden_two)
    out_two = normed_two * perceptron_layernorm_scale + perceptron_layernorm_offset
    member_f = member.astype(jnp.float32)
    counts = piece_sizes.astype(jnp.float32)[..., None]
    pooled = (
        jnp.einsum(
            "rsl,rld->rsd",
            member_f,
            out_two.reshape(rows_here, length, width),
            precision=FULL_ACCURACY,
        )
        / counts
    )
    inv_norm = lax.rsqrt(jnp.sum(pooled * pooled, axis=-1, keepdims=True) + EPS_UNIT)
    units = pooled * inv_norm
    units_low = units.astype(jnp.bfloat16)
    question_directions = units_low[:, 0::2].reshape(rows_here * half, width)
    passage_directions = units_low[:, 1::2].reshape(rows_here * half, width)
    all_passages = lax.all_gather(passage_directions, ("gx", "gy"), axis=0, tiled=True)
    total_docs = all_passages.shape[0]
    cosine_score_table = (
        reduce_along_second_axis(question_directions, all_passages) / softmax_sharpness[0]
    )
    sim_top = jnp.max(cosine_score_table, axis=1, keepdims=True)
    sim_exp = jnp.exp(cosine_score_table - sim_top)
    sim_total = jnp.sum(sim_exp, axis=1, keepdims=True)
    log_total = sim_top[:, 0] + jnp.log(sim_total[:, 0])
    chosen = matching_passage_number[:, None] == jnp.arange(total_docs, dtype=jnp.int32)[None, :]
    positive = jnp.sum(jnp.where(chosen, cosine_score_table, 0.0), axis=1)
    local_loss = jnp.sum(log_total - positive)
    cosine_score_derivative = (sim_exp / sim_total - chosen.astype(jnp.float32)) / total_docs
    cotangent_times_jacobian = (cosine_score_derivative / softmax_sharpness[0]).astype(jnp.bfloat16)
    grad_query_units = jnp.dot(
        cotangent_times_jacobian, all_passages, preferred_element_type=jnp.float32
    )
    grad_doc_units = lax.psum_scatter(
        contract_rows(cotangent_times_jacobian, question_directions),
        ("gx", "gy"),
        scatter_dimension=0,
        tiled=True,
    )
    grad_units = jnp.stack(
        [
            grad_query_units.reshape(rows_here, half, width),
            grad_doc_units.reshape(rows_here, half, width),
        ],
        axis=2,
    ).reshape(rows_here, segments, width)
    along = jnp.sum(units * grad_units, axis=-1, keepdims=True)
    grad_pooled = inv_norm * (grad_units - units * along)
    grad_out_two = jnp.einsum(
        "rsl,rsd->rld", member_f, grad_pooled / counts, precision=FULL_ACCURACY
    ).reshape(count_tokens, width)
    grad_gain_ffn = jnp.sum(grad_out_two * normed_two, axis=0)
    grad_shift_ffn = jnp.sum(grad_out_two, axis=0)
    grad_hidden_two = standardize_back(
        normed_two, inv_two, grad_out_two * perceptron_layernorm_scale
    )
    grad_branch_two = grad_hidden_two.astype(jnp.bfloat16)
    grad_b_outer = jnp.sum(grad_branch_two, axis=0, dtype=jnp.float32)
    grad_w_outer = contract_rows(inner_low, grad_branch_two)
    grad_act = reduce_along_second_axis(grad_branch_two, narrowing_projection)
    grad_pre = (grad_act * gelu_slope(inner_pre)).astype(jnp.bfloat16)
    grad_b_inner = jnp.sum(grad_pre, axis=0, dtype=jnp.float32)
    grad_w_inner = contract_rows(out_one_low, grad_pre)
    ffn_list = (
        grad_w_inner,
        grad_b_inner,
        grad_w_outer,
        grad_b_outer,
        grad_gain_ffn,
        grad_shift_ffn,
    )
    ffn_summed = []
    grad_out_one = grad_hidden_two + reduce_along_second_axis(grad_pre, widening_projection)
    grad_gain_attn = jnp.sum(grad_out_one * normed_one, axis=0)
    grad_shift_attn = jnp.sum(grad_out_one, axis=0)
    grad_hidden_one = standardize_back(normed_one, inv_one, grad_out_one * mixing_layernorm_scale)
    grad_branch_one = grad_hidden_one.astype(jnp.bfloat16)
    grad_b_output = jnp.sum(grad_branch_one, axis=0, dtype=jnp.float32)
    grad_w_output = contract_rows(attn_flat, grad_branch_one)
    grad_attn = reduce_along_second_axis(grad_branch_one, mixing_result_projection).astype(
        jnp.bfloat16
    )
    grad_q_rows, grad_k_rows, grad_v_rows = lax.map(
        attend_back,
        (query_rows, key_rows, value_rows, token_seg, lse_rows, grad_attn.reshape(head_shape)),
    )
    grad_queries = grad_q_rows.reshape(count_tokens, width)
    grad_keys = grad_k_rows.reshape(count_tokens, width)
    grad_values = grad_v_rows.reshape(count_tokens, width)
    grad_b_query = jnp.sum(grad_queries, axis=0, dtype=jnp.float32)
    grad_b_value = jnp.sum(grad_values, axis=0, dtype=jnp.float32)
    grad_w_query = contract_rows(flat_tokens, grad_queries)
    grad_w_key = contract_rows(flat_tokens, grad_keys)
    grad_w_value = contract_rows(flat_tokens, grad_values)
    grad_tokens = (
        grad_hidden_one
        + reduce_along_second_axis(grad_queries, question_projection)
        + reduce_along_second_axis(grad_keys, lookup_projection)
        + reduce_along_second_axis(grad_values, content_projection)
    )
    attn_list = (
        grad_w_query,
        grad_b_query,
        grad_w_key,
        grad_w_value,
        grad_b_value,
        grad_w_output,
        grad_b_output,
        grad_gain_attn,
        grad_shift_attn,
    )
    main_list = attn_list + ffn_list
    summed, loss_total = reduce_main(pack(main_list, width), local_loss)
    results = unpack(summed, main_list, width) + list(ffn_summed)
    loss_out = (loss_total / total_docs).reshape(1)
    return (loss_out, pooled, grad_tokens.reshape(rows_here, length, width)) + tuple(results)


def solution(mesh):
    return jax.shard_map(
        body,
        mesh=mesh,
        in_specs=(
            P(("gx", "gy"), None, None),
            P(("gx", "gy"), None),
            P(("gx", "gy")),
            P(),
            P(),
            P(),
            P(),
            P(),
            P(),
            P(),
            P(),
            P(),
            P(),
            P(),
            P(),
            P(),
            P(),
            P(),
            P(),
        ),
        out_specs=(
            P(),
            P(("gx", "gy"), None, None),
            P(("gx", "gy"), None, None),
            P("gy", None),
            P("gy"),
            P("gy", None),
            P("gy", None),
            P("gy"),
            P("gy", None),
            P("gy"),
            P("gy"),
            P("gy"),
            P("gy", None),
            P("gy"),
            P("gy", None),
            P("gy"),
            P("gy"),
            P("gy"),
        ),
        check_vma=False,
    )
```

profile of v0, /device:TPU:0, one launch (start us, length us, event | category | flops | bytes accessed | tf_op | source)
XLA Modules:
  0.0 683.8 jit_solution(16935765170544003585)
XLA Ops:
  7.3 0.9 reduce_window_sum.11
  8.2 1.2 convert_bitcast_fusion
  9.4 1.3 convert_element_type.154
  10.7 1.3 convert_element_type.152
  13.4 2.4 add_convert_fusion.1
  15.7 1.2 copy.107
  17.0 0.9 broadcast_compare_fusion
  17.9 2.0 add_convert_fusion
  20.3 3.2 convolution_convert_fusion.1
  23.5 1.4 copy.109
  25.6 3.6 fusion.22
  29.2 3.8 fusion
  33.8 5.2 fusion.29
  39.1 0.9 fusion.93
  40.5 19.5 %fusion.4 = (bf16[512,3072]{1,0:T(8,128)(2,1)S(1)}, f32[512,3072]{1,0:T(8,128)}) fusion(f32[3072]{0:T(1024)S(1)} %copy-done.38, bf16[768,3072]{1,0:T(8,128)(2,1)} %param.32, f32[512,768]{1,0:T(8,128)S(1)} %get-tuple-element.102, f32[768]{0:T(1024)S(1)} %copy-done.53, f32[768]{0:T(1024)S(1)} %convert_element_type.149, f32[512]{0:T(512)S(1)} %add_rsqrt_fusion.1, ...), kind=kOutput, calls=%fused_computation.12 | convolution fusion | flops 2521694208 | bytes 15751168 | tf_op jit(solution)/shard_map/dot_general | solution.py:193
  60.1 2.8 fusion.94
  63.3 1.0 multiply_reduce_fusion.10
  67.7 44.3 %all-gather = bf16[1,128,768]{2,0,1:T(2,128)(2,1)S(1)} all-gather(bf16[1,4,768]{2,0,1:T(2,128)(2,1)S(1)} %copy.111), channel_id=2, replica_groups=mesh['gx'=2,'gy'=16] {'gx','gy'}, dimensions={1}, use_global_device_ids=true | all-gather | bytes 202752 | tf_op jit(solution)/shard_map/all_gather | solution.py:220
  112.7 1.0 fusion.95
  113.7 1.4 fusion.75
  115.6 1.8 fusion.71
  117.4 1.9 convolution_bitcast_fusion
  119.3 1.4 log_add_fusion
  120.7 120.6 %all-reduce.5.cloned.1.call-done = f32[128,768]{1,0:T(8,128)} async-done(((f32[128,768]{1,0:T(8,128)}), f32[128,768]{1,0:T(8,128)}) %all-reduce.5.cloned.1.call-update) | async-done | bytes 393232
  243.4 1.4 reshape.459
  244.7 0.9 multiply_reduce_fusion.9
  245.7 2.8 multiply_reduce_fusion.1
  249.2 9.0 %convert_reduce_fusion = (f32[3072]{0:T(1024)}, bf16[512,3072]{1,0:T(8,128)(2,1)S(1)}) fusion(f32[512,3072]{1,0:T(8,128)} %get-tuple-element.104, f32[3072]{0:T(1024)S(1)} %copy-done.39, bf16[3072,768]{1,0:T(8,128)(2,1)} %param.34, f32[512,768]{1,0:T(8,128)S(1)} %get-tuple-element.88), kind=kOutput, calls=%fused_computation.20 | convolution fusion | flops 2436756480 | bytes 15753216 | tf_op jit(solution)/shard_map/dot_general | solution.py:50
  258.3 3.6 multiply_reduce_fusion.2
  261.9 1.1 convert_reduce_fusion.2
  263.0 1.7 convolution_convert_fusion
  264.7 1.4 copy.113
  266.2 12.1 %multiply_reduce_fusion = (f32[12,512]{1,0:T(8,128)S(1)}, f32[12,512,512]{1,2,0:T(8,128)}) fusion(f32[12,512]{1,0:T(8,128)} %log_add_fusion, f32[12,512,512]{1,2,0:T(8,128)} %copy-done.2, pred[512,512]{0,1:T(8,128)(4,1)} %broadcast_compare_fusion, bf16[512,12,64]{0,2,1:T(8,128)(2,1)S(1)} %bitcast.135, bf16[512,12,64]{0,2,1:T(8,128)(2,1)} %bitcast.134), kind=kOutput, calls=%fused_computation.1 | convolution fusion | flops 418375680 | bytes 27049984 | tf_op jit(solution)/shard_map/while/body/eval_jaxpr/qhd,khd->hqk/dot_general | solution.py:82
  278.3 7.1 %multiply_convert_fusion = bf16[12,512,512]{1,2,0:T(8,128)(2,1)S(1)} fusion(f32[12,512,512]{1,2,0:T(8,128)} %get-tuple-element.114, f32[12,512]{1,0:T(8,128)S(1)} %get-tuple-element.113, f32[12,512]{1,0:T(8,128)S(1)} %copy-done.27, f32[12,512,512]{1,2,0:T(8,128)S(1)} %bitcast.120, pred[512,512]{0,1:T(8,128)(4,1)S(1)} %copy-done.8), kind=kLoop, calls=%fused_computation | loop fusion | flops 18874368 | bytes 31768576 | tf_op jit(solution)/shard_map/while/body/eval_jaxpr/convert_element_type | solution.py:86
  285.4 2.9 multiply_convert_fusion.1
  288.3 1.2 convert_reduce_fusion.4
  289.6 4.9 convert_reduce_fusion.3
  294.5 5.6 fusion.87
  300.1 5.1 fusion.78
  305.2 2.2 fusion.40
  307.8 2.2 fusion.38
  310.0 2.3 fusion.36
  312.3 1.1 concatenate.48
  313.4 3.3 fusion.34
  317.0 1.0 concatenate.50
  318.0 1.0 concatenate.51
  319.0 1.8 concatenate.41
  320.9 11.4 %concatenate.42 = f32[16,2,24,3072]{3,2,1,0:T(8,128)} reshape(f32[3072,768]{1,0:T(8,128)} %fusion.78) | data formatting | bytes 18874368 | tf_op jit(solution)/shard_map/concatenate | solution.py:124
  332.3 1.0 concatenate.52
  333.3 1.0 concatenate.53
  334.4 1.0 concatenate.54
  335.4 36.2 %concatenate.46 = f32[16,2,24,9228]{3,2,1,0:T(8,128)} concatenate(f32[16,2,24,768]{3,2,1,0:T(8,128)} %bitcast.126, f32[16,2,24,1]{3,2,1,0:T(8,128)S(1)} %concatenate.47, f32[16,2,24,768]{3,2,1,0:T(8,128)} %bitcast.127, f32[16,2,24,768]{3,2,1,0:T(8,128)} %bitcast.128, f32[16,2,24,1]{3,2,1,0:T(8,128)S(1)} %concatenate.48, f32[16,2,24,768]{3,2,1,0:T(8,128)} %fusion.34, ...), dimensions={3} | concatenate | bytes 56696832 | tf_op jit(solution)/shard_map/concatenate | solution.py:124
  371.6 20.1 %copy.125 = f32[2,16,24,9228]{3,2,1,0:T(8,128)} copy(f32[2,16,24,9228]{3,2,0,1:T(8,128)} %bitcast.122) | data formatting | bytes 56696832 | tf_op jit(solution)/shard_map/transpose | solution.py:105
  393.7 39.5 %all-reduce = f32[32]{0:T(128)S(1)} all-reduce(f32[32]{0:T(128)S(1)} %broadcast_in_dim.58), channel_id=3, replica_groups=mesh['gx'=2,'gy'=16] {'gx','gy'}, use_global_device_ids=true, to_apply=%region_13.14.clone | all-reduce | flops 32 | bytes 256
  434.5 2.4 fusion.97
  436.8 0.8 fusion.96
  437.7 2.1 add_bitcast_fusion
  439.8 217.2 %reduce-scatter.4.cloned.1.call-done = f32[24,9228]{1,0:T(8,128)} async-done(((f32[768,9228]{1,0:T(8,128)}), f32[24,9228]{1,0:T(8,128)}) %reduce-scatter.4.cloned.1.call-update) | async-done | bytes 885904
  657.0 1.2 convert_element_type.179
  658.2 12.5 %all_gather.7 = bf16[48,9228]{1,0:T(8,128)(2,1)S(1)} all-gather(bf16[24,9228]{1,0:T(8,128)(2,1)S(1)} %convert_element_type.179), channel_id=1, replica_groups=mesh['gx'=2,'gy'=16] {'gx'}, dimensions={0}, use_global_device_ids=true | all-gather | bytes 1328832 | tf_op jit(solution)/shard_map/all_gather | solution.py:119
  670.7 0.9 fusion.92
  671.7 1.0 fusion.91
  672.9 0.8 slice_reduce_fusion
  674.4 1.0 reshape.471
  (200 shorter events, 14.6 us)
Async XLA Ops:
  7.2 31.8 %copy-start = (bf16[768,768]{1,0:T(8,128)(2,1)S(1)}, bf16[768,768]{1,0:T(8,128)(2,1)}, u32[]{:S(2)}) copy-start(bf16[768,768]{1,0:T(8,128)(2,1)} %param.28) | copy-start | bytes 3538948
  7.2 234.1 %all-reduce.5.cloned.1.call-start = ((), (), s32[]{:S(2)}) async-start(), calls=%async_computation.1 | async-start | bytes 786432
  8.2 9.7 %copy-start.62 = (s32[1,8]{1,0:T(1,128)}, s32[1,8]{1,0:T(1,128)S(1)}, u32[]{:S(2)}) copy-start(s32[1,8]{1,0:T(1,128)S(1)} %reduce_window_sum.11) | copy-start | bytes 100
  9.4 8.5 %copy-start.64 = (s32[8]{0:T(128)}, s32[8]{0:T(128)S(1)}, u32[]{:S(2)}) copy-start(s32[8]{0:T(128)S(1)} %get-tuple-element.98) | copy-start | bytes 100
  13.4 4.6 copy-start.57
  13.4 4.6 copy-start.5
  20.0 4.9 copy-start.58
  20.0 5.5 copy-start.59
  20.3 8.9 %copy-start.3 = (bf16[512,768]{0,1:T(8,128)(2,1)}, bf16[512,768]{0,1:T(8,128)(2,1)S(1)}, u32[]{:S(2)}) copy-start(bf16[512,768]{0,1:T(8,128)(2,1)S(1)} %copy.108) | copy-start | bytes 2359300
  25.6 34.5 %copy-start.33 = (f32[768]{0:T(1024)}, f32[768]{0:T(1024)S(1)}, u32[]{:S(2)}) copy-start(f32[768]{0:T(1024)S(1)} %convert_element_type.149) | copy-start | bytes 9220
  29.2 4.6 copy-start.2
  29.2 4.6 copy-start.7
  29.2 4.6 copy-start.26
  33.0 6.0 copy-start.28
  39.1 21.0 %slice-start.3 = ((s8[4718592]{0:T(1024)(128)(4,1)}), s8[524288]{0:T(1024)(128)(4,1)S(1)}, s32[]{:S(2)}) async-start(s8[4718592]{0:T(1024)(128)(4,1)} %bitcast.147), calls=%async_computation.6 | async-start | bytes 1048576
  40.0 20.0 %copy-start.13 = (f32[512,768]{1,0:T(8,128)}, f32[512,768]{1,0:T(8,128)S(1)}, u32[]{:S(2)}) copy-start(f32[512,768]{1,0:T(8,128)S(1)} %get-tuple-element.102) | copy-start | bytes 4718596
  40.4 19.7 %copy-start.40 = (f32[512]{0:T(512)}, f32[512]{0:T(512)S(1)}, u32[]{:S(2)}) copy-start(f32[512]{0:T(512)S(1)} %add_rsqrt_fusion.1) | copy-start | bytes 6148
  40.4 22.9 %copy-start.36 = (f32[768]{0:T(1024)}, f32[768]{0:T(1024)S(1)}, u32[]{:S(2)}) copy-start(f32[768]{0:T(1024)S(1)} %convert_element_type.155) | copy-start | bytes 9220
  40.4 19.6 %copy-start.55 = (f32[768]{0:T(1024)S(1)}, f32[768]{0:T(1024)}, u32[]{:S(2)}) copy-start(f32[768]{0:T(1024)} %convert_element_type.154) | copy-start | bytes 9220
  40.5 19.6 %slice-start.4 = ((s8[4718592]{0:T(1024)(128)(4,1)}), s8[4194304]{0:T(1024)(128)(4,1)S(1)}, s32[]{:S(2)}) async-start(s8[4718592]{0:T(1024)(128)(4,1)} %bitcast.147), calls=%async_computation.7 | async-start | bytes 8388608
  60.0 2.9 copy-start.18
  60.1 3.2 copy-start.63
  60.1 3.2 copy-start.65
  60.1 3.2 copy-start.67
  63.0 1.4 copy-start.30
  66.3 182.2 %copy-start.31 = (f32[512]{0:T(512)S(1)}, f32[512]{0:T(512)}, u32[]{:S(2)}) copy-start(f32[512]{0:T(512)} %copy-done.30) | copy-start | bytes 6148
  66.3 182.2 %copy-start.37 = (f32[768]{0:T(1024)S(1)}, f32[768]{0:T(1024)}, u32[]{:S(2)}) copy-start(f32[768]{0:T(1024)} %copy-done.36) | copy-start | bytes 9220
  117.4 539.6 %reduce-scatter.4.cloned.1.call-start = ((), (), s32[]{:S(2)}) async-start(), calls=%async_computation.2 | async-start | bytes 29601792
  244.7 3.8 copy-start.44
  248.5 9.7 %slice-start.5 = ((s8[4718592]{0:T(1024)(128)(4,1)}), s8[4194304]{0:T(1024)(128)(4,1)S(1)}, s32[]{:S(2)}) async-start(s8[4718592]{0:T(1024)(128)(4,1)} %bitcast.149), calls=%async_computation.8 | async-start | bytes 8388608
  249.1 9.2 %copy-start.11 = (f32[512,768]{1,0:T(8,128)}, f32[512,768]{1,0:T(8,128)S(1)}, u32[]{:S(2)}) copy-start(f32[512,768]{1,0:T(8,128)S(1)} %get-tuple-element.88) | copy-start | bytes 4718596
  249.2 9.0 %copy-start.14 = (f32[512,768]{1,0:T(8,128)S(1)}, f32[512,768]{1,0:T(8,128)}, u32[]{:S(2)}) copy-start(f32[512,768]{1,0:T(8,128)} %copy-done.13) | copy-start | bytes 4718596
  249.2 9.0 %copy-start.34 = (f32[768]{0:T(1024)S(1)}, f32[768]{0:T(1024)}, u32[]{:S(2)}) copy-start(f32[768]{0:T(1024)} %copy-done.33) | copy-start | bytes 9220
  249.2 9.0 %copy-start.41 = (f32[512]{0:T(512)S(1)}, f32[512]{0:T(512)}, u32[]{:S(2)}) copy-start(f32[512]{0:T(512)} %copy-done.40) | copy-start | bytes 6148
  249.2 9.0 %slice-start.6 = ((s8[4718592]{0:T(1024)(128)(4,1)}), s8[524288]{0:T(1024)(128)(4,1)S(1)}, s32[]{:S(2)}) async-start(s8[4718592]{0:T(1024)(128)(4,1)} %bitcast.149), calls=%async_computation.9 | async-start | bytes 1048576
  258.2 3.7 copy-start.69
  266.2 12.1 %copy-start.16 = (bf16[512,768]{0,1:T(8,128)(2,1)}, bf16[512,768]{0,1:T(8,128)(2,1)S(1)}, u32[]{:S(2)}) copy-start(bf16[512,768]{0,1:T(8,128)(2,1)S(1)} %copy.113) | copy-start | bytes 2359300
  266.2 12.1 %slice-start = ((s8[12582912]{0:T(1024)(128)(4,1)}), s8[4194304]{0:T(1024)(128)(4,1)S(1)}, s32[]{:S(2)}) async-start(s8[12582912]{0:T(1024)(128)(4,1)} %bitcast.119), calls=%async_computation.3 | async-start | bytes 8388608
  266.2 12.1 %slice-start.1 = ((s8[12582912]{0:T(1024)(128)(4,1)}), s8[4194304]{0:T(1024)(128)(4,1)S(1)}, s32[]{:S(2)}) async-start(s8[12582912]{0:T(1024)(128)(4,1)} %bitcast.119), calls=%async_computation.4 | async-start | bytes 8388608
  266.2 12.1 %slice-start.2 = ((s8[12582912]{0:T(1024)(128)(4,1)}), s8[4194304]{0:T(1024)(128)(4,1)S(1)}, s32[]{:S(2)}) async-start(s8[12582912]{0:T(1024)(128)(4,1)} %bitcast.119), calls=%async_computation.5 | async-start | bytes 8388608
  266.2 12.1 %copy-start.8 = (pred[512,512]{0,1:T(8,128)(4,1)S(1)}, pred[512,512]{0,1:T(8,128)(4,1)}, u32[]{:S(2)}) copy-start(pred[512,512]{0,1:T(8,128)(4,1)} %broadcast_compare_fusion) | copy-start | bytes 786436
  266.2 12.1 %copy-start.27 = (f32[12,512]{1,0:T(8,128)S(1)}, f32[12,512]{1,0:T(8,128)}, u32[]{:S(2)}) copy-start(f32[12,512]{1,0:T(8,128)} %log_add_fusion) | copy-start | bytes 73732
  278.3 7.1 %copy-start.4 = (bf16[512,768]{0,1:T(8,128)(2,1)S(1)}, bf16[512,768]{0,1:T(8,128)(2,1)}, u32[]{:S(2)}) copy-start(bf16[512,768]{0,1:T(8,128)(2,1)} %copy-done.3) | copy-start | bytes 2359300
  289.5 15.7 %copy-start.9 = (bf16[12,64,512]{2,1,0:T(8,128)(2,1)}, bf16[12,64,512]{2,1,0:T(8,128)(2,1)S(1)}, u32[]{:S(2)}) copy-start(bf16[12,64,512]{2,1,0:T(8,128)(2,1)S(1)} %get-tuple-element.116) | copy-start | bytes 2359300
  289.5 4.9 copy-start.15
  289.5 4.9 copy-start.35
  289.5 4.9 copy-start.42
  289.5 4.9 copy-start.54
  289.6 4.9 copy-start.70
  294.5 5.6 copy-start.12
  294.5 5.6 copy-start.19
  300.1 5.1 copy-start.6
  305.2 2.6 copy-start.20
  307.8 2.2 copy-start.21
  312.3 4.4 copy-start.32
  312.3 4.7 copy-start.52
  312.3 5.7 copy-start.51
  320.9 12.5 %copy-start.50 = (f32[768]{0:T(1024)S(1)}, f32[768]{0:T(1024)}, u32[]{:S(2)}) copy-start(f32[768]{0:T(1024)} %get-tuple-element.69) | copy-start | bytes 9220
  320.9 13.5 %copy-start.49 = (f32[768]{0:T(1024)S(1)}, f32[768]{0:T(1024)}, u32[]{:S(2)}) copy-start(f32[768]{0:T(1024)} %get-tuple-element.83) | copy-start | bytes 9220
  391.7 45.1 %copy-start.10 = (bf16[12,64,512]{2,1,0:T(8,128)(2,1)S(1)}, bf16[12,64,512]{2,1,0:T(8,128)(2,1)}, u32[]{:S(2)}) copy-start(bf16[12,64,512]{2,1,0:T(8,128)(2,1)} %copy-done.9) | copy-start | bytes 2359300
  433.2 3.6 copy-start.68
  434.4 3.2 copy-start.22
  434.4 3.2 copy-start.23
  670.7 4.6 copy-start.1
  (16 other events, 15.5 us)
Sparse Core Ops, SparseCore 0:
  117.5 123.7 all-reduce.4
  391.9 265.0 reduce-scatter.3
where the time goes:
time: 692 us; the launch traced here: 684 us
  waiting for transfers between devices  338 us (49%)
  matrix products  110 us (16%)
  blocking collectives  96.4 us (14%)
  local copies, waits for them, and re-layouts  94.7 us (14%)
  other arithmetic  27.2 us (4%)
  between operations  18 us (3%)
    unnamed x4, waiting for transfers between devices  338 us
    concatenate x11, local copies, waits for them, and re-layouts, pack(): jnp.concatenate([entry.reshape(width, -1) for entry in entries], axis=1)  56.3 us
    all_gather x1, blocking collectives, body(): lax.all_gather(passage_directions, ('gx', 'gy'), axis=0, tiled=True)  44.3 us
    unnamed x1, blocking collectives  39.5 us
    dot_general x7, matrix products, contract_rows(): lax.dot_general(left, right, (((0,), (0,)), ((), ())), preferred_element_...  22.5 us
    dot_general x7, matrix products, reduce_along_second_axis(): lax.dot_general(left, right, (((1,), (1,)), ((), ())), preferred_element_...  20.6 us
    transpose x1, local copies, waits for them, and re-layouts, arrange(): view = jnp.swapaxes(view.reshape(groups_y, groups_x, sub, columns), 0, 1)  20.1 us
    dot_general x1, matrix products, body(): jnp.dot(out_one_low, widening_projection, preferred_element_type=jnp.floa...  19.5 us
  transfers between devices with their start and end apart: 2, of which 2 were waited for; matrix products, arithmetic and copies ran while one was open for 2% of the time, Pallas kernels for 0%

commit v1 on v0

v1 whole, which is shorter than its diff:
```python
import functools

import jax
import jax.numpy as jnp
import numpy as np
from jax import lax
from jax.experimental import pallas as pl
from jax.experimental.pallas import tpu as pltpu
from jax.sharding import PartitionSpec as P

HEADS = 12
HD = 64
LANES = 128
VMEM_BYTES = 60 * 1024 * 1024

EPS_NORM = 1e-12
EPS_UNIT = 1e-06
NEG_FILL = -1e30


def standardize(hidden):
    center = hidden - jnp.mean(hidden, axis=-1, keepdims=True)
    inv_scale = lax.rsqrt(jnp.mean(center * center, axis=-1, keepdims=True) + EPS_NORM)
    return (center * inv_scale, inv_scale)


def standardize_back(normed, inv_scale, grad_normed):
    mean_grad = jnp.mean(grad_normed, axis=-1, keepdims=True)
    mean_both = jnp.mean(grad_normed * normed, axis=-1, keepdims=True)
    return inv_scale * (grad_normed - mean_grad - normed * mean_both)


def widen(value):
    return value.astype(jnp.float32)


def powers_below(count):
    bits = []
    bit = 1
    while bit < count:
        bits.append(bit)
        bit *= 2
    return bits


def place_masks(bits):
    masks = [0]
    for bit in reversed(bits):
        masks = masks + [mask ^ bit for mask in masks]
    return masks


def swap_with(value, axis, bit):
    count = lax.axis_size(axis)
    return lax.ppermute(value, axis, [(i, i ^ bit) for i in range(count)])


def tie(*values):
    return lax.optimization_barrier(values)


def gather_steps():
    gy = powers_below(lax.axis_size("gy"))
    far = [("gy", bit) for bit in reversed(gy[2:])]
    near = [("gy", bit) for bit in reversed(gy[:2])]
    return far + [("gx", bit) for bit in powers_below(lax.axis_size("gx"))] + near


def gather_blocks(block, beside):
    groups_y = lax.axis_size("gy")
    gathered = block[None]
    number = np.zeros((1,), np.int32)
    place = 0
    for step, (axis, bit) in enumerate(gather_steps()):
        if step == 3:
            gathered, beside = tie(gathered, beside)
        gathered = jnp.concatenate([gathered, swap_with(gathered, axis, bit)], axis=0)
        high = (lax.axis_index(axis) & bit) != 0
        number = np.concatenate([number, number + bit * (groups_y if axis == "gx" else 1)])
        place = place + jnp.where(high, 1 << step, 0)
    return gathered, number, place, beside


def add_halves(keep, got):
    half = keep.shape[0] // 2
    kept = widen(keep[:half]) + widen(got[:half])
    return kept, (widen(keep[half:]) + widen(got[half:])).astype(jnp.bfloat16)


def swap_sum(current, axis, bit):
    mine = current.astype(jnp.bfloat16)
    return widen(mine) + widen(swap_with(mine, axis, bit))


def sum_over_gx(current, bits):
    for bit in bits:
        current = swap_sum(current, "gx", bit)
    return current


def finish_shares(keep, got, bits):
    for bit in bits:
        keep, send = add_halves(keep, got)
        got = swap_with(send, "gy", bit)
    return widen(keep[0]) + widen(got[0])


def gather_over_gx(mine):
    mine = mine.astype(jnp.bfloat16)
    other = swap_with(mine, "gx", 1)
    high = (lax.axis_index("gx") & 1) != 0
    return widen(
        jnp.concatenate([jnp.where(high, other, mine), jnp.where(high, mine, other)], axis=0)
    )


def halve_row(current, bit):
    half = current.shape[0] // 2
    lower, upper = current[:half], current[half:]
    high = (lax.axis_index("gy") & bit) != 0
    received = swap_with(jnp.where(high, lower, upper), "gy", bit)
    return jnp.where(high, upper, lower) + received


def share_of(blocks, columns):
    tiles = columns // LANES
    count, rows, _ = blocks.shape
    parts = count // tiles
    view = blocks.reshape(tiles, parts, rows, LANES)
    return view.transpose(1, 2, 0, 3).reshape(parts * rows, columns)


def compiler_params():
    return pltpu.CompilerParams(vmem_limit_bytes=VMEM_BYTES)


def dot_nt(left, right):
    return lax.dot_general(
        left, right, (((1,), (1,)), ((), ())), preferred_element_type=jnp.float32
    )


def dot_nn(left, right):
    return jnp.dot(left, right, preferred_element_type=jnp.float32)


def start_all(copies):
    for copy in copies:
        copy.start()


def wait_all(copies):
    for copy in copies:
        copy.wait()


def as_row(ref):
    return ref[...].astype(jnp.float32).reshape(1, ref.shape[0])


def lengths_as_row(sizes_ref, lanes, segments):
    lane = lax.broadcasted_iota(jnp.int32, (1, lanes), 1) % segments
    start = jnp.zeros((1, lanes), jnp.int32)
    end = jnp.zeros((1, lanes), jnp.int32)
    at = jnp.int32(0)
    for segment in range(segments):
        size = sizes_ref[0, segment]
        start = jnp.where(lane == segment, at, start)
        at = at + size
        end = jnp.where(lane == segment, at, end)
    return start, end


def counts_as_column(sizes_ref, segments):
    row = lax.broadcasted_iota(jnp.int32, (segments, 1), 0)
    counts = jnp.zeros((segments, 1), jnp.float32)
    for segment in range(segments):
        counts = jnp.where(row == segment, sizes_ref[0, segment].astype(jnp.float32), counts)
    return counts


def starts_as_column(sizes_ref, segments):
    row = lax.broadcasted_iota(jnp.int32, (segments, 1), 0)
    start = jnp.zeros((segments, 1), jnp.int32)
    end = jnp.zeros((segments, 1), jnp.int32)
    at = jnp.int32(0)
    for segment in range(segments):
        size = sizes_ref[0, segment]
        start = jnp.where(row == segment, at, start)
        at = at + size
        end = jnp.where(row == segment, at, end)
    return start, end


def band(length):
    return [(0, length // 2, 0, 3 * length // 4), (length // 2, length, length // 4, length)]


def mask_of(sizes_ref, segments, query_at, query_end, key_at, key_end):
    query = query_at + lax.broadcasted_iota(jnp.int32, (1, query_end - query_at), 1)
    low = jnp.zeros_like(query)
    high = jnp.zeros_like(query)
    at = jnp.int32(0)
    for segment in range(segments):
        end = at + sizes_ref[0, segment]
        inside = (query >= at) & (query < end)
        low = jnp.where(inside, at, low)
        high = jnp.where(inside, end, high)
        at = end
    padding = query >= at
    low = jnp.where(padding, at, low)
    high = jnp.where(padding, key_end, high)
    key = key_at + lax.broadcasted_iota(jnp.int32, (key_end - key_at, query_end - query_at), 0)
    return jnp.where((key >= low) & (key < high), 0.0, NEG_FILL)


def vmem_spec():
    return pl.BlockSpec(memory_space=pltpu.VMEM)


def smem_spec():
    return pl.BlockSpec(memory_space=pltpu.SMEM)


def any_spec():
    return pl.BlockSpec(memory_space=pltpu.HBM)


def cost(microseconds):
    return pl.CostEstimate(
        flops=int(microseconds * 1.1e9), bytes_accessed=1000000, transcendentals=0
    )


def forward_kernel(segments, masks_x, masks_z, here_ref, sizes_ref, matching_ref, *refs):
    given, refs = refs[:16], refs[16:]
    results, refs = refs[:14], refs[14:]
    side_own, side_send = results[-2:]
    local, refs = refs[:16], refs[16:]
    made, refs = refs[:12], refs[12:]
    (
        tokens_ref,
        question_w,
        lookup_w,
        content_w,
        mixing_w,
        widening_w,
        narrowing_w,
        question_row,
        content_row,
        mixing_row,
        gain_one_row,
        shift_one_row,
        widening_row,
        narrowing_row,
        gain_two_row,
        shift_two_row,
    ) = local
    (
        query_ref,
        key_ref,
        key_t_ref,
        value_ref,
        lse_ref,
        normed_one_ref,
        inv_one_ref,
        slope_ref,
        normed_two_ref,
        inv_two_ref,
        pooled_ref,
        message_ref,
    ) = made
    value_t, token_t, attn_t, out_one_t, inner_t, fill = refs[:6]
    out_one, out_one_low, total, in_sems, out_sems, side_sems = refs[6:]
    length, width = tokens_ref.shape
    hidden_units = widening_w.shape[1]
    here = here_ref[0]
    share_rows = side_own.shape[1] // (hidden_units // width + 3)
    inner_rows = hidden_units // width * share_rows
    first_rows = inner_rows // 2
    copies = [
        pltpu.make_async_copy(source, target, in_sems.at[i])
        for i, (source, target) in enumerate(zip(given, local))
    ]
    outward = [
        pltpu.make_async_copy(source, target, out_sems.at[i])
        for i, (source, target) in enumerate(zip(made, results))
    ]
    side_copies = []

    def send_side(source, source_rows, offset, count, at, masks):
        for place, mask in enumerate(masks):
            for flip, target in enumerate((side_own, side_send)):
                share = jnp.bitwise_xor(here, mask ^ flip)
                first = pl.multiple_of(share * source_rows + offset, 8)
                copy = pltpu.make_async_copy(
                    source.at[pl.ds(first, count)],
                    target.at[place, pl.ds(at, count)],
                    side_sems.at[len(side_copies)],
                )
                copy.start()
                side_copies.append(copy)

    start_all(copies)
    ranges = band(length)
    for i, (query_at, query_end, key_at, key_end) in enumerate(ranges):
        fill[i] = mask_of(sizes_ref, segments, query_at, query_end, key_at, key_end)
    wait_all(copies[7:])
    copies[0].wait()
    token_t[...] = tokens_ref[...].T
    send_side(token_t, share_rows, 0, share_rows, inner_rows + share_rows, masks_x)
    wide = 2 * LANES
    copies[1].wait()
    for at in range(0, width, wide):
        product = dot_nn(tokens_ref[...], question_w[:, at : at + wide])
        product = (product + as_row(question_row)[:, at : at + wide]).astype(jnp.bfloat16)
        query_ref[:, at : at + wide] = product * jnp.bfloat16(HD ** (-0.5))
    copies[2].wait()
    for at in range(0, width, wide):
        product = dot_nn(tokens_ref[...], lookup_w[:, at : at + wide]).astype(jnp.bfloat16)
        key_ref[:, at : at + wide] = product
        key_t_ref[at : at + wide, :] = product.T
    copies[3].wait()
    for at in range(0, width, wide):
        product = dot_nn(tokens_ref[...], content_w[:, at : at + wide])
        product = (product + as_row(content_row)[:, at : at + wide]).astype(jnp.bfloat16)
        value_ref[:, at : at + wide] = product
        value_t[at : at + wide, :] = product.T
    start_all(outward[:4])
    lane = lax.broadcasted_iota(jnp.int32, (1, LANES), 1)
    for pair in range(width // LANES):
        lanes = slice(pair * LANES, (pair + 1) * LANES)
        for i, (query_at, query_end, key_at, key_end) in enumerate(ranges):
            keys = key_ref[key_at:key_end, lanes]
            for which in range(LANES // HD):
                at = pair * (LANES // HD) + which
                query = jnp.where((lane // HD) == which, query_ref[query_at:query_end, lanes], 0)
                scores = dot_nt(keys, query) + fill[i]
                top = jnp.max(scores, axis=0, keepdims=True)
                expo = jnp.exp(scores - top)
                norm = jnp.sum(expo, axis=0, keepdims=True)
                probs = (expo * (1.0 / norm)).astype(jnp.bfloat16)
                lse_ref[at : at + 1, query_at:query_end] = top + jnp.log(norm)
                mixed = dot_nn(value_t[at * HD : (at + 1) * HD, key_at:key_end], probs)
                attn_t[at * HD : (at + 1) * HD, query_at:query_end] = mixed.astype(
                    jnp.bfloat16
                )
    outward[4].start()
    send_side(attn_t, share_rows, 0, share_rows, inner_rows + 2 * share_rows, masks_x)
    copies[4].wait()
    chunk = min(length, 128)
    for at in range(0, length, chunk):
        rows = slice(at, at + chunk)
        hidden = (
            tokens_ref[rows].astype(jnp.float32)
            + dot_nn(attn_t[:, rows].T, mixing_w[...])
            + as_row(mixing_row)
        )
        normed, inv = standardize(hidden)
        normed_one_ref[rows] = normed
        inv_one_ref[rows] = inv
        shifted = normed * as_row(gain_one_row) + as_row(shift_one_row)
        out_one[rows] = shifted
        low = shifted.astype(jnp.bfloat16)
        out_one_low[rows] = low
        out_one_t[:, rows] = low.T
        total[rows] = shifted + as_row(narrowing_row)
    start_all(outward[5:7])
    send_side(out_one_t, share_rows, 0, share_rows, inner_rows, masks_x)
    copies[5].wait()
    copies[6].wait()
    tile = 2 * LANES

    def widen_tile(step, carry):
        at = pl.multiple_of(step * tile, tile)
        inner_parts = []
        for row in range(0, length, chunk):
            rows = slice(row, row + chunk)
            before = (
                dot_nn(out_one_low[rows], widening_w[:, pl.ds(at, tile)])
                + widening_row[pl.ds(at, tile)].astype(jnp.float32).reshape(1, tile)
            )
            cdf = 0.5 * (1.0 + lax.erf(before * 0.7071067811865476))
            pdf = jnp.exp(-0.5 * before * before) * 0.3989422804014327
            inner = (before * cdf).astype(jnp.bfloat16)
            slope_ref[rows, pl.ds(at, tile)] = (cdf + before * pdf).astype(jnp.bfloat16)
            inner_t[pl.ds(at, tile), rows] = inner.T
            total[rows] += dot_nn(inner, narrowing_w[pl.ds(at, tile), :])
        return carry

    lax.fori_loop(0, hidden_units // tile, widen_tile, 0)
    outward[7].start()
    send_side(inner_t, inner_rows, 0, first_rows, 0, masks_x)
    send_side(inner_t, inner_rows, first_rows, inner_rows - first_rows, first_rows, masks_z)
    start, end = starts_as_column(sizes_ref, segments)
    sums = jnp.zeros((segments, width), jnp.float32)
    for at in range(0, length, chunk):
        rows = slice(at, at + chunk)
        normed, inv = standardize(total[rows])
        normed_two_ref[rows] = normed
        inv_two_ref[rows] = inv
        out_two = normed * as_row(gain_two_row) + as_row(shift_two_row)
        upper = out_two.astype(jnp.bfloat16)
        lower = (out_two - upper.astype(jnp.float32)).astype(jnp.bfloat16)
        token = at + lax.broadcasted_iota(jnp.int32, (segments, chunk), 1)
        member = jnp.where((token >= start) & (token < end), 1.0, 0.0).astype(jnp.bfloat16)
        sums = sums + dot_nn(member, upper) + dot_nn(member, lower)
    pooled = sums / counts_as_column(sizes_ref, segments)
    pooled_ref[...] = pooled
    inv_norm = lax.rsqrt(jnp.sum(pooled * pooled, axis=1, keepdims=True) + EPS_UNIT)
    units = (pooled * inv_norm).astype(jnp.bfloat16)
    half = segments // 2
    place = lax.broadcasted_iota(jnp.int32, (segments, segments), 0)
    source = lax.broadcasted_iota(jnp.int32, (segments, segments), 1)
    wanted = jnp.where(place < half, 2 * place, 2 * (place - half) + 1)
    pick = jnp.where(source == wanted, 1.0, 0.0).astype(jnp.bfloat16)
    message_ref[:, :width] = dot_nn(pick, units).astype(jnp.bfloat16)
    row = lax.broadcasted_iota(jnp.int32, (segments, LANES), 0)
    column = lax.broadcasted_iota(jnp.int32, (segments, LANES), 1)
    digits = jnp.zeros((segments, LANES), jnp.float32)
    for i in range(half):
        number = matching_ref[i]
        digit = jnp.where(column == 0, number & 255, number >> 8).astype(jnp.float32)
        digits = jnp.where((row == i) & (column < 2), digit, digits)
    message_ref[:, width:] = digits.astype(jnp.bfloat16)
    start_all(outward[8:])
    wait_all(outward)
    wait_all(side_copies)


def forward_step(here, sizes, matching, masks_x, masks_z, given):
    tokens, hidden_units = given[0], given[5].shape[1]
    length, width = tokens.shape
    segments = sizes.shape[1]
    half = len(masks_x)
    query_at, query_end, key_at, key_end = band(length)[0]
    low, full = jnp.bfloat16, jnp.float32
    side = ((half, (hidden_units // width + 3) * (width // half // 2), length), low)
    made = [
        ((length, width), low),
        ((length, width), low),
        ((width, length), low),
        ((length, width), low),
        ((HEADS, length), full),
        ((length, width), full),
        ((length, 1), full),
        ((length, hidden_units), low),
        ((length, width), full),
        ((length, 1), full),
        ((segments, width), full),
        ((segments, width + LANES), low),
    ]
    return pl.pallas_call(
        functools.partial(forward_kernel, segments, masks_x, masks_z),
        in_specs=[smem_spec()] * 3 + [any_spec()] * len(given),
        out_specs=[any_spec()] * (len(made) + 2),
        out_shape=[jax.ShapeDtypeStruct(shape, kind) for shape, kind in made + [side, side]],
        scratch_shapes=[pltpu.VMEM(item.shape, item.dtype) for item in given]
        + [pltpu.VMEM(shape, kind) for shape, kind in made]
        + [
            pltpu.VMEM((width, length), low),
            pltpu.VMEM((width, length), low),
            pltpu.VMEM((width, length), low),
            pltpu.VMEM((width, length), low),
            pltpu.VMEM((hidden_units, length), low),
            pltpu.VMEM((2, key_end - key_at, query_end - query_at), full),
            pltpu.VMEM((length, width), full),
            pltpu.VMEM((length, width), low),
            pltpu.VMEM((length, width), full),
            pltpu.SemaphoreType.DMA((len(given),)),
            pltpu.SemaphoreType.DMA((len(made),)),
            pltpu.SemaphoreType.DMA((2 * 5 * half,)),
        ],
        compiler_params=compiler_params(),
        cost_estimate=cost(28),
        name="forward_step",
    )(here, sizes, matching, *given)


def loss_kernel(
    place_ref,
    sizes_ref,
    sharpness_ref,
    numbers_ref,
    gathered_hbm,
    pooled_hbm,
    normed_hbm,
    inv_hbm,
    gain_hbm,
    loss_ref,
    grad_hidden_hbm,
    grad_branch_hbm,
    sums_ref,
    gathered_ref,
    pooled_ref,
    normed_ref,
    inv_ref,
    gain_ref,
    grad_hidden_ref,
    grad_branch_ref,
    sems,
):
    given = [
        (gathered_hbm, gathered_ref),
        (pooled_hbm, pooled_ref),
        (normed_hbm, normed_ref),
        (inv_hbm, inv_ref),
        (gain_hbm, gain_ref),
    ]
    copies = [
        pltpu.make_async_copy(source, target, sems.at[i])
        for i, (source, target) in enumerate(given)
    ]
    start_all(copies)
    segments, width = pooled_ref.shape
    half = segments // 2
    devices = gathered_ref.shape[0]
    total = devices * half
    sharpness = sharpness_ref[0]
    row = lax.broadcasted_iota(jnp.int32, (total, devices * segments), 0)
    column = lax.broadcasted_iota(jnp.int32, (total, devices * segments), 1)
    source = jnp.bitwise_xor(row // half, place_ref[0]) * segments + row % half
    copies[0].wait()
    gathered = gathered_ref[...].reshape(devices * segments, width + LANES)
    pick = jnp.where(column == source, 1.0, 0.0).astype(jnp.bfloat16)
    picked = dot_nn(pick, gathered)
    questions = picked[:, :width].astype(jnp.bfloat16)
    digits = picked[:, width:]
    pick = jnp.where(column == source + half, 1.0, 0.0).astype(jnp.bfloat16)
    passages = dot_nn(pick, gathered[:, :width]).astype(jnp.bfloat16)
    matching = (digits[:, 0:1] + 256.0 * digits[:, 1:2]).astype(jnp.int32)
    table = dot_nt(questions, passages) / sharpness
    top = jnp.max(table, axis=1, keepdims=True)
    expo = jnp.exp(table - top)
    expo_total = jnp.sum(expo, axis=1, keepdims=True)
    chosen = matching == numbers_ref[...]
    positive = jnp.sum(jnp.where(chosen, table, 0.0), axis=1, keepdims=True)
    loss_ref[...] = (
        jnp.sum(top + jnp.log(expo_total) - positive, axis=0, keepdims=True) / total
    )
    slope = (expo / expo_total - chosen.astype(jnp.float32)) / total
    grad_dot = (slope / sharpness).astype(jnp.bfloat16)
    segment_at = lax.broadcasted_iota(jnp.int32, (segments, total), 0)
    column = lax.broadcasted_iota(jnp.int32, (segments, total), 1)
    mine = column == place_ref[0] * half + segment_at // 2
    is_query = segment_at % 2 == 0
    pick_query = jnp.where(mine & is_query, 1.0, 0.0).astype(jnp.bfloat16)
    pick_passage = jnp.where(mine & ~is_query, 1.0, 0.0).astype(jnp.bfloat16)
    row_terms = dot_nn(pick_query, grad_dot).astype(jnp.bfloat16)
    column_terms = dot_nt(pick_passage, grad_dot).astype(jnp.bfloat16)
    grad_units = dot_nn(row_terms, passages) + dot_nn(column_terms, questions)
    wait_all(copies[1:])
    pooled = pooled_ref[...]
    inv_norm = lax.rsqrt(jnp.sum(pooled * pooled, axis=1, keepdims=True) + EPS_UNIT)
    units = pooled * inv_norm
    along = jnp.sum(units * grad_units, axis=1, keepdims=True)
    grad_pooled = inv_norm * (grad_units - units * along) / counts_as_column(sizes_ref, segments)
    upper = grad_pooled.astype(jnp.bfloat16)
    lower = (grad_pooled - upper.astype(jnp.float32)).astype(jnp.bfloat16)
    both = jnp.concatenate([upper, lower], axis=0)
    start, end = lengths_as_row(sizes_ref, 2 * segments, segments)
    gain = as_row(gain_ref)
    outward = []
    tokens = normed_ref.shape[0]
    chunk = min(tokens, 128)
    gain_sum = jnp.zeros((1, width), jnp.float32)
    shift_sum = jnp.zeros((1, width), jnp.float32)
    bias_sum = jnp.zeros((1, width), jnp.float32)
    for at in range(0, tokens, chunk):
        token = at + lax.broadcasted_iota(jnp.int32, (chunk, 2 * segments), 0)
        member = jnp.where((token >= start) & (token < end), 1.0, 0.0).astype(jnp.bfloat16)
        grad_out = dot_nn(member, both)
        normed = normed_ref[at : at + chunk]
        gain_sum = gain_sum + jnp.sum(grad_out * normed, axis=0, keepdims=True)
        shift_sum = shift_sum + jnp.sum(grad_out, axis=0, keepdims=True)
        grad_hidden = standardize_back(normed, inv_ref[at : at + chunk], grad_out * gain)
        grad_hidden_ref[at : at + chunk] = grad_hidden
        low = grad_hidden.astype(jnp.bfloat16)
        grad_branch_ref[at : at + chunk] = low
        bias_sum = bias_sum + jnp.sum(low.astype(jnp.float32), axis=0, keepdims=True)
        for source_ref, target in (
            (grad_hidden_ref, grad_hidden_hbm),
            (grad_branch_ref, grad_branch_hbm),
        ):
            copy = pltpu.make_async_copy(
                source_ref.at[at : at + chunk],
                target.at[at : at + chunk],
                sems.at[len(copies) + len(outward)],
            )
            copy.start()
            outward.append(copy)
    sums_ref[...] = jnp.concatenate([bias_sum, gain_sum, shift_sum], axis=0)
    wait_all(outward)


def loss_step(place, sizes, sharpness, numbers, gathered, pooled, normed, inv, gain):
    tokens, width = normed.shape
    low, full = jnp.bfloat16, jnp.float32
    chunks = -(-tokens // 128)
    return pl.pallas_call(
        loss_kernel,
        in_specs=[smem_spec()] * 3 + [vmem_spec()] + [any_spec()] * 5,
        out_specs=[vmem_spec(), any_spec(), any_spec(), vmem_spec()],
        out_shape=[
            jax.ShapeDtypeStruct((1, 1), full),
            jax.ShapeDtypeStruct((tokens, width), full),
            jax.ShapeDtypeStruct((tokens, width), low),
            jax.ShapeDtypeStruct((3, width), full),
        ],
        scratch_shapes=[
            pltpu.VMEM(gathered.shape, low),
            pltpu.VMEM(pooled.shape, full),
            pltpu.VMEM(normed.shape, full),
            pltpu.VMEM(inv.shape, full),
            pltpu.VMEM(gain.shape, low),
            pltpu.VMEM((tokens, width), full),
            pltpu.VMEM((tokens, width), low),
            pltpu.SemaphoreType.DMA((5 + 2 * chunks,)),
        ],
        compiler_params=compiler_params(),
        cost_estimate=cost(4),
        name="loss_step",
    )(place, sizes, sharpness, numbers, gathered, pooled, normed, inv, gain)


def before_kernel(branch_ref, slope_ref, narrowing_ref, grad_pre_ref, bias_ref):
    tokens = slope_ref.shape[0]
    chunk = min(tokens, 256)
    bias = jnp.zeros((1, slope_ref.shape[1]), jnp.float32)
    for at in range(0, tokens, chunk):
        grad_act = dot_nt(branch_ref[at : at + chunk], narrowing_ref[...])
        grad_pre = (grad_act * widen(slope_ref[at : at + chunk])).astype(jnp.bfloat16)
        grad_pre_ref[at : at + chunk] = grad_pre
        bias = bias + jnp.sum(widen(grad_pre), axis=0, keepdims=True)
    bias_ref[...] = bias


def before_step(branch, slope, narrowing):
    tokens, hidden_units = slope.shape
    width = branch.shape[1]
    tile = 4 * LANES
    return pl.pallas_call(
        before_kernel,
        grid=(hidden_units // tile,),
        in_specs=[
            pl.BlockSpec((tokens, width), lambda i: (0, 0)),
            pl.BlockSpec((tokens, tile), lambda i: (0, i)),
            pl.BlockSpec((tile, width), lambda i: (i, 0)),
        ],
        out_specs=[
            pl.BlockSpec((tokens, tile), lambda i: (0, i)),
            pl.BlockSpec((1, tile), lambda i: (0, i)),
        ],
        out_shape=[
            jax.ShapeDtypeStruct((tokens, hidden_units), jnp.bfloat16),
            jax.ShapeDtypeStruct((1, hidden_units), jnp.float32),
        ],
        compiler_params=compiler_params(),
        cost_estimate=cost(6),
        name="before_step",
    )(branch, slope, narrowing)


def side_copies(own_ref, other_ref, at, count, target, sems):
    tokens = own_ref.shape[2]
    return [
        pltpu.make_async_copy(
            source.at[:, pl.ds(at, count)],
            target.at[:, :, pl.ds(i * tokens, tokens)],
            sems.at[i],
        )
        for i, source in enumerate((own_ref, other_ref))
    ]


def flat(ref):
    places, rows, tokens = ref.shape
    return ref[...].reshape(places * rows, tokens)


def store_shares(product, parts, at, keep, send):
    rows = keep.shape[2]
    low = product.astype(jnp.bfloat16)
    for place in range(low.shape[0] // rows // parts):
        target = keep if place < keep.shape[0] else send
        for tile in range(low.shape[1] // LANES):
            for part in range(parts):
                row = (place * parts + part) * rows
                target[place % keep.shape[0], at + tile * parts + part] = low[
                    row : row + rows, tile * LANES : (tile + 1) * LANES
                ]


def outer_kernel(
    own_ref,
    other_ref,
    branch_own_ref,
    branch_other_ref,
    keep_x,
    send_x,
    keep_z,
    send_z,
    left_x,
    left_z,
    sems,
):
    count = left_x.shape[1]
    parts = count // keep_x.shape[2]
    copies_x = side_copies(own_ref, other_ref, 0, count, left_x, sems.at[0])
    copies_z = side_copies(own_ref, other_ref, count, count, left_z, sems.at[1])
    first = pl.program_id(0) == 0

    @pl.when(first)
    def _():
        start_all(copies_x + copies_z)
        wait_all(copies_x)

    right = jnp.concatenate([branch_own_ref[...], branch_other_ref[...]], axis=0)
    store_shares(dot_nn(flat(left_x), right), parts, 0, keep_x, send_x)

    @pl.when(first)
    def _():
        wait_all(copies_z)

    store_shares(dot_nn(flat(left_z), right), parts, 0, keep_z, send_z)


def outer_step(own, other, branch_own, branch_other, count):
    places, _, tokens = own.shape
    width = branch_own.shape[1]
    wide = 2 * LANES
    parts = 2
    rows = count // parts
    shape = jax.ShapeDtypeStruct(
        (places // 2, width // LANES * parts, rows, LANES), jnp.bfloat16
    )
    column = pl.BlockSpec((tokens, wide), lambda i: (0, i))
    return pl.pallas_call(
        outer_kernel,
        grid=(width // wide,),
        in_specs=[any_spec(), any_spec(), column, column],
        out_specs=[pl.BlockSpec((places // 2, 2 * parts, rows, LANES), lambda i: (0, i, 0, 0))]
        * 4,
        out_shape=[shape] * 4,
        scratch_shapes=[
            pltpu.VMEM((places, count, 2 * tokens), jnp.bfloat16),
            pltpu.VMEM((places, count, 2 * tokens), jnp.bfloat16),
            pltpu.SemaphoreType.DMA((2, 2)),
        ],
        compiler_params=compiler_params(),
        cost_estimate=cost(6),
        name="outer_step",
    )(own, other, branch_own, branch_other)


def inner_kernel(
    at,
    side_ref,
    own_ref,
    other_ref,
    grad_own_ref,
    grad_other_ref,
    widening_ref,
    hidden_hbm,
    normed_hbm,
    inv_hbm,
    gain_hbm,
    mixing_hbm,
    keep_ref,
    send_ref,
    grad_hidden_ref,
    grad_branch_ref,
    grad_attn_ref,
    sums_ref,
    left,
    total,
    normed_ref,
    inv_ref,
    gain_ref,
    mixing_ref,
    side_sems,
    sems,
):
    step = pl.program_id(0)
    steps = pl.num_programs(0)
    first = step == 0
    left_copies = side_copies(own_ref, other_ref, at, left.shape[1], left, side_sems)
    given = [
        (hidden_hbm, total),
        (normed_hbm, normed_ref),
        (inv_hbm, inv_ref),
        (gain_hbm, gain_ref),
        (mixing_hbm, mixing_ref),
    ]
    copies = [
        pltpu.make_async_copy(source, target, sems.at[i])
        for i, (source, target) in enumerate(given)
    ]

    @pl.when(first)
    def _():
        start_all(left_copies + copies)
        wait_all(left_copies)
        copies[0].wait()

    tokens = grad_own_ref.shape[0]
    product = dot_nn(flat(left)[:, :tokens], grad_own_ref[...]) + dot_nn(
        flat(left)[:, tokens:], grad_other_ref[...]
    )

    @pl.when(step < steps // 2)
    def _():
        store_shares(product, 1, 0, keep_ref, keep_ref)

    @pl.when(step >= steps // 2)
    def _():
        store_shares(product, 1, 0, send_ref, send_ref)

    total[...] += dot_nt(grad_own_ref[...], widening_ref[...])

    @pl.when(step == steps - 1)
    def _():
        wait_all(copies[1:])
        width = normed_ref.shape[1]
        chunk = min(tokens, 128)
        gain = as_row(gain_ref)
        gain_sum = jnp.zeros((1, width), jnp.float32)
        shift_sum = jnp.zeros((1, width), jnp.float32)
        bias_sum = jnp.zeros((1, width), jnp.float32)
        for row in range(0, tokens, chunk):
            grad_out = total[row : row + chunk]
            normed = normed_ref[row : row + chunk]
            gain_sum = gain_sum + jnp.sum(grad_out * normed, axis=0, keepdims=True)
            shift_sum = shift_sum + jnp.sum(grad_out, axis=0, keepdims=True)
            grad_hidden = standardize_back(normed, inv_ref[row : row + chunk], grad_out * gain)
            grad_hidden_ref[row : row + chunk] = grad_hidden
            low = grad_hidden.astype(jnp.bfloat16)
            grad_branch_ref[row : row + chunk] = low
            bias_sum = bias_sum + jnp.sum(widen(low), axis=0, keepdims=True)
            grad_attn_ref[row : row + chunk] = dot_nt(low, mixing_ref[...]).astype(jnp.bfloat16)
        sums_ref[...] = jnp.concatenate([bias_sum, gain_sum, shift_sum], axis=0)


def inner_step(
    side, own, other, at, rows, grad_own, grad_other, widening, hidden, normed, inv, gain, mixing
):
    places, _, tokens = own.shape
    width = normed.shape[1]
    hidden_units = grad_own.shape[1]
    tile = 4 * LANES
    steps = hidden_units // tile
    low, full = jnp.bfloat16, jnp.float32
    shape = jax.ShapeDtypeStruct((places, hidden_units // LANES // 2, rows, LANES), low)
    block = (places, tile // LANES, rows, LANES)

    def tile_of(i, side):
        return (i + side[0] * (steps // 2)) % steps

    def whole(kind):
        return pl.BlockSpec((tokens, width), lambda i, side: (0, 0))

    return pl.pallas_call(
        functools.partial(inner_kernel, at),
        grid_spec=pltpu.PrefetchScalarGridSpec(
            num_scalar_prefetch=1,
            grid=(steps,),
            in_specs=[
                any_spec(),
                any_spec(),
                pl.BlockSpec((tokens, tile), lambda i, side: (0, tile_of(i, side))),
                pl.BlockSpec((tokens, tile), lambda i, side: (0, tile_of(i, side))),
                pl.BlockSpec((width, tile), lambda i, side: (0, tile_of(i, side))),
                any_spec(),
                any_spec(),
                any_spec(),
                any_spec(),
                any_spec(),
            ],
            out_specs=[
                pl.BlockSpec(block, lambda i, side: (0, jnp.minimum(i, steps // 2 - 1), 0, 0)),
                pl.BlockSpec(block, lambda i, side: (0, jnp.maximum(i - steps // 2, 0), 0, 0)),
                whole(full),
                whole(low),
                whole(low),
                pl.BlockSpec((3, width), lambda i, side: (0, 0)),
            ],
            scratch_shapes=[
                pltpu.VMEM((places, rows, 2 * tokens), low),
                pltpu.VMEM((tokens, width), full),
                pltpu.VMEM(normed.shape, full),
                pltpu.VMEM(inv.shape, full),
                pltpu.VMEM(gain.shape, low),
                pltpu.VMEM(mixing.shape, low),
                pltpu.SemaphoreType.DMA((2,)),
                pltpu.SemaphoreType.DMA((5,)),
            ],
        ),
        out_shape=[
            shape,
            shape,
            jax.ShapeDtypeStruct((tokens, width), full),
            jax.ShapeDtypeStruct((tokens, width), low),
            jax.ShapeDtypeStruct((tokens, width), low),
            jax.ShapeDtypeStruct((3, width), full),
        ],
        compiler_params=compiler_params(),
        cost_estimate=cost(12),
        name="inner_step",
    )(side, own, other, grad_own, grad_other, widening, hidden, normed, inv, gain, mixing)


def attend_back_kernel(
    segments,
    sizes_ref,
    query_ref,
    key_ref,
    key_t_ref,
    value_ref,
    lse_ref,
    grad_ref,
    grads_ref,
    sums_ref,
    fill,
    query_t,
    total_key,
    total_value,
):
    length, wide = query_ref.shape
    ranges = band(length)
    step = pl.program_id(0)

    @pl.when(step == 0)
    def _():
        for i, (query_at, query_end, key_at, key_end) in enumerate(ranges):
            fill[i] = mask_of(sizes_ref, segments, query_at, query_end, key_at, key_end)

    total_key[...] = jnp.zeros_like(total_key)
    total_value[...] = jnp.zeros_like(total_value)
    lane = lax.broadcasted_iota(jnp.int32, (1, LANES), 1)
    for pair in range(wide // LANES):
        lanes = slice(pair * LANES, (pair + 1) * LANES)
        for i, (query_at, query_end, key_at, key_end) in enumerate(ranges):
            keys = key_ref[key_at:key_end, lanes]
            values = value_ref[key_at:key_end, lanes]
            grad_key = None
            grad_value = None
            for which in range(LANES // HD):
                head = (lane // HD) == which
                query = jnp.where(head, query_ref[query_at:query_end, lanes], 0)
                grad = jnp.where(head, grad_ref[query_at:query_end, lanes], 0)
                at = pair * (LANES // HD) + which
                scores = dot_nt(keys, query) + fill[i]
                probs = jnp.exp(scores - lse_ref[0, at : at + 1, query_at:query_end])
                grad_probs = dot_nt(values, grad)
                inner = jnp.sum(grad_probs * probs, axis=0, keepdims=True)
                grad_scores = (probs * (grad_probs - inner)).astype(jnp.bfloat16)
                value_term = dot_nn(probs.astype(jnp.bfloat16), grad)
                key_term = dot_nn(grad_scores, query)
                query_t[at * HD : (at + 1) * HD, query_at:query_end] = dot_nn(
                    key_t_ref[at * HD : (at + 1) * HD, key_at:key_end], grad_scores
                )
                grad_key = key_term if grad_key is None else grad_key + key_term
                grad_value = value_term if grad_value is None else grad_value + value_term
            total_key[key_at:key_end, lanes] += grad_key
            total_value[key_at:key_end, lanes] += grad_value
    grad_query = (query_t[...] * HD ** (-0.5)).T.astype(jnp.bfloat16)
    grad_value = total_value[...].astype(jnp.bfloat16)
    grads_ref[0] = grad_query
    grads_ref[1] = total_key[...].astype(jnp.bfloat16)
    grads_ref[2] = grad_value
    sums_ref[...] = jnp.concatenate(
        [
            jnp.sum(widen(grad_query), axis=0, keepdims=True),
            jnp.sum(widen(grad_value), axis=0, keepdims=True),
        ],
        axis=0,
    )


def attend_back_step(sizes, query, key, key_t, value, lse, grad):
    tokens, width = query.shape
    heads_here = lse.shape[1]
    wide = heads_here * HD
    columns = pl.BlockSpec((tokens, wide), lambda i: (0, i))
    query_at, query_end, key_at, key_end = band(tokens)[0]
    return pl.pallas_call(
        functools.partial(attend_back_kernel, sizes.shape[1]),
        grid=(width // wide,),
        in_specs=[
            smem_spec(),
            columns,
            columns,
            pl.BlockSpec((wide, tokens), lambda i: (i, 0)),
            columns,
            pl.BlockSpec((1, heads_here, tokens), lambda i: (i, 0, 0)),
            columns,
        ],
        out_specs=[
            pl.BlockSpec((3, tokens, wide), lambda i: (0, 0, i)),
            pl.BlockSpec((2, wide), lambda i: (0, i)),
        ],
        out_shape=[
            jax.ShapeDtypeStruct((3, tokens, width), jnp.bfloat16),
            jax.ShapeDtypeStruct((2, width), jnp.float32),
        ],
        scratch_shapes=[
            pltpu.VMEM((2, key_end - key_at, query_end - query_at), jnp.float32),
            pltpu.VMEM((wide, tokens), jnp.float32),
            pltpu.VMEM((tokens, wide), jnp.float32),
            pltpu.VMEM((tokens, wide), jnp.float32),
        ],
        compiler_params=compiler_params(),
        cost_estimate=cost(12),
        name="attend_back_step",
    )(sizes, query, key, key_t, value, lse, grad)


def token_kernel(hidden_ref, grads_ref, question_ref, lookup_ref, content_ref, out_ref):
    out_ref[...] = (
        hidden_ref[...]
        + dot_nt(grads_ref[0], question_ref[...])
        + dot_nt(grads_ref[1], lookup_ref[...])
        + dot_nt(grads_ref[2], content_ref[...])
    )


def token_step(hidden, grads, question, lookup, content):
    tokens, width = hidden.shape
    wide = 2 * LANES
    weight = pl.BlockSpec((wide, width), lambda i: (i, 0))
    column = pl.BlockSpec((tokens, wide), lambda i: (0, i))
    return pl.pallas_call(
        token_kernel,
        grid=(width // wide,),
        in_specs=[column, pl.BlockSpec((3, tokens, width), lambda i: (0, 0, 0))] + [weight] * 3,
        out_specs=column,
        out_shape=jax.ShapeDtypeStruct((tokens, width), jnp.float32),
        compiler_params=compiler_params(),
        cost_estimate=cost(5),
        name="token_step",
    )(hidden, grads, question, lookup, content)


def attention_kernel(
    token_at,
    attn_at,
    side_ref,
    own_ref,
    other_ref,
    grads_own_ref,
    grads_other_ref,
    branch_own_ref,
    branch_other_ref,
    keep_x,
    send_x,
    keep_y,
    send_y,
    token_left,
    attn_left,
    sems,
):
    first = pl.program_id(0) == 0
    rows = token_left.shape[1]
    copies = side_copies(own_ref, other_ref, token_at, rows, token_left, sems.at[0])
    copies = copies + side_copies(own_ref, other_ref, attn_at, rows, attn_left, sems.at[1])

    @pl.when(first)
    def _():
        start_all(copies)
        wait_all(copies)

    side = side_ref[0]

    def both(index):
        return jnp.concatenate([grads_own_ref[index], grads_other_ref[index]], axis=0)

    token = flat(token_left)
    store_shares(dot_nn(token, both(0)), 1, 0, keep_x.at[:, 0], send_x.at[:, 0])
    branch = jnp.concatenate([branch_own_ref[...], branch_other_ref[...]], axis=0)
    store_shares(dot_nn(flat(attn_left), branch), 1, 0, keep_x.at[:, 1], send_x.at[:, 1])
    store_shares(dot_nn(token, both(1 + side)), 1, 0, keep_y, keep_y)
    store_shares(dot_nn(token, both(2 - side)), 1, 0, send_y, send_y)


def attention_step(
    side, own, other, token_at, attn_at, rows, grads_own, grads_other, branch_own, branch_other
):
    places, _, tokens = own.shape
    width = branch_own.shape[1]
    wide = 2 * LANES
    tiles = width // LANES
    low = jnp.bfloat16
    shape_x = jax.ShapeDtypeStruct((places // 2, 2, tiles, rows, LANES), low)
    shape_y = jax.ShapeDtypeStruct((places, tiles, rows, LANES), low)
    block_x = pl.BlockSpec((places // 2, 2, 2, rows, LANES), lambda i: (0, 0, i, 0, 0))
    block_y = pl.BlockSpec((places, 2, rows, LANES), lambda i: (0, i, 0, 0))
    grads = pl.BlockSpec((3, tokens, wide), lambda i: (0, 0, i))
    column = pl.BlockSpec((tokens, wide), lambda i: (0, i))
    return pl.pallas_call(
        functools.partial(attention_kernel, token_at, attn_at),
        grid=(width // wide,),
        in_specs=[smem_spec(), any_spec(), any_spec(), grads, grads, column, column],
        out_specs=[block_x, block_x, block_y, block_y],
        out_shape=[shape_x, shape_x, shape_y, shape_y],
        scratch_shapes=[
            pltpu.VMEM((places, rows, 2 * tokens), low),
            pltpu.VMEM((places, rows, 2 * tokens), low),
            pltpu.SemaphoreType.DMA((2, 2)),
        ],
        compiler_params=compiler_params(),
        cost_estimate=cost(5),
        name="attention_step",
    )(side, own, other, grads_own, grads_other, branch_own, branch_other)


def body(
    hidden_states_in,
    piece_sizes,
    matching_passage_number,
    softmax_sharpness,
    question_projection,
    question_offset,
    lookup_projection,
    content_projection,
    content_offset,
    mixing_result_projection,
    mixing_result_offset,
    mixing_layernorm_scale,
    mixing_layernorm_offset,
    widening_projection,
    widening_offset,
    narrowing_projection,
    narrowing_offset,
    perceptron_layernorm_scale,
    perceptron_layernorm_offset,
):
    rows_here, length, width = hidden_states_in.shape
    segments = piece_sizes.shape[1]
    per_device = segments // 2
    groups_y = lax.axis_size("gy")
    tiles = width // LANES
    rows = width // groups_y
    inner_rows = widening_offset.shape[0] // groups_y
    gy_bits = powers_below(groups_y)
    order_x = gy_bits[1:]
    order_z = gy_bits[2:] + gy_bits[1:2]
    here = lax.axis_index("gy").astype(jnp.int32).reshape(1)
    side = (lax.axis_index("gx").astype(jnp.int32) & 1).reshape(1)
    (
        queries,
        keys,
        keys_t,
        values,
        lse,
        normed_one,
        inv_one,
        slope,
        normed_two,
        inv_two,
        pooled,
        message,
        side_own,
        side_send,
    ) = forward_step(
        here,
        piece_sizes,
        matching_passage_number,
        place_masks(order_x),
        place_masks(order_z),
        [
            hidden_states_in[0],
            question_projection,
            lookup_projection,
            content_projection,
            mixing_result_projection,
            widening_projection,
            narrowing_projection,
            question_offset,
            content_offset,
            mixing_result_offset,
            mixing_layernorm_scale,
            mixing_layernorm_offset,
            widening_offset,
            narrowing_offset,
            perceptron_layernorm_scale,
            perceptron_layernorm_offset,
        ],
    )
    gathered, numbers_of, place, side_other = gather_blocks(
        message, swap_with(side_send, "gy", 1)
    )
    numbers = (numbers_of[:, None] * per_device + np.arange(per_device)[None, :]).reshape(1, -1)
    loss_out, grad_hidden_two, branch_two, sums_two = loss_step(
        place.astype(jnp.int32).reshape(1),
        piece_sizes,
        softmax_sharpness,
        jnp.asarray(numbers, jnp.int32),
        gathered,
        pooled,
        normed_two,
        inv_two,
        perceptron_layernorm_scale,
    )
    branch_two_other = swap_with(branch_two, "gy", 1)
    grad_pre, grad_b_inner = before_step(branch_two, slope, narrowing_projection)
    branch_two_other, grad_pre = tie(branch_two_other, grad_pre)
    grad_pre_other = swap_with(grad_pre, "gy", 1)
    outer_keep_x, outer_send_x, outer_keep_z, outer_send_z = outer_step(
        side_own, side_other, branch_two, branch_two_other, inner_rows // 2
    )
    grad_pre_other, outer_send_x, outer_send_z = tie(grad_pre_other, outer_send_x, outer_send_z)
    outer_got_x = swap_with(outer_send_x, "gy", order_x[0])
    outer_got_z = swap_with(outer_send_z, "gy", order_z[0])
    inner_keep, inner_send, grad_hidden_one, branch_one, grad_attn, sums_one = inner_step(
        side,
        side_own,
        side_other,
        inner_rows,
        rows,
        grad_pre,
        grad_pre_other,
        widening_projection,
        grad_hidden_two,
        normed_one,
        inv_one,
        mixing_layernorm_scale,
        mixing_result_projection,
    )
    gx_bits = powers_below(lax.axis_size("gx"))
    outer_got_x, outer_got_z, branch_one, inner_send = tie(
        outer_got_x, outer_got_z, branch_one, inner_send
    )
    outer_keep_x, outer_send_x = add_halves(outer_keep_x, outer_got_x)
    outer_keep_z, outer_send_z = add_halves(outer_keep_z, outer_got_z)
    inner_got = swap_with(inner_send, "gx", 1)
    outer_got_x = swap_with(outer_send_x, "gy", order_x[1])
    outer_got_z = swap_with(outer_send_z, "gy", order_z[1])
    branch_one_other = swap_with(branch_one, "gy", 1)
    heads_at_once = 4
    grads, sums_attn = attend_back_step(
        piece_sizes,
        queries,
        keys,
        keys_t,
        values,
        lse.reshape(HEADS // heads_at_once, heads_at_once, length),
        grad_attn,
    )
    branch_one_other, grads = tie(branch_one_other, grads)
    grads_other = swap_with(grads, "gy", 1)
    grad_tokens = token_step(
        grad_hidden_one, grads, question_projection, lookup_projection, content_projection
    )
    grads_other, grad_tokens = tie(grads_other, grad_tokens)
    attn_keep_x, attn_send_x, attn_keep_y, attn_send_y = attention_step(
        side,
        side_own,
        side_other,
        inner_rows + rows,
        inner_rows + 2 * rows,
        rows,
        grads,
        grads_other,
        branch_one,
        branch_one_other,
    )
    outer_got_x, outer_got_z, attn_send_x, attn_send_y, sums_attn = tie(
        outer_got_x, outer_got_z, attn_send_x, attn_send_y, sums_attn
    )
    attn_got_x = swap_with(attn_send_x, "gy", order_x[0])
    attn_got_y = swap_with(attn_send_y, "gx", 1)
    vectors = jnp.concatenate([sums_attn, sums_one, sums_two], axis=0)
    vectors = vectors.reshape(8, groups_y, rows).transpose(1, 0, 2).reshape(groups_y, 8 * rows)
    vectors = jnp.concatenate([vectors, grad_b_inner.reshape(groups_y, -1)], axis=1)
    for bit in reversed(gy_bits):
        vectors = halve_row(vectors, bit)
    for bit in gx_bits:
        vectors = vectors + swap_with(vectors, "gx", bit)
    vector_sums = vectors[0]
    b_query, b_value, b_output, gain_attn, shift_attn, b_outer, gain_ffn, shift_ffn = [
        vector_sums[i * rows : (i + 1) * rows] for i in range(8)
    ]
    outer_x = finish_shares(outer_keep_x, outer_got_x, order_x[2:])
    outer_z = finish_shares(outer_keep_z, outer_got_z, order_z[2:])
    outer_both = sum_over_gx(jnp.concatenate([outer_x, outer_z], axis=0), gx_bits)
    outer_x, outer_z = jnp.split(outer_both, 2, axis=0)
    attn_x = finish_shares(attn_keep_x, attn_got_x, order_x[1:])
    attn_x = sum_over_gx(attn_x, gx_bits)
    keep = jnp.concatenate([inner_keep, attn_keep_y], axis=1)
    got = jnp.concatenate([inner_got, attn_got_y], axis=1)
    both_y = finish_shares(keep, got, order_x)
    both_y = sum_over_gx(both_y, gx_bits[1:])
    split_at = inner_keep.shape[1]
    both_y = gather_over_gx(both_y).reshape((2,) + both_y.shape)
    inner_sums = both_y[:, :split_at].reshape((-1,) + both_y.shape[2:])
    attn_y = both_y[:, split_at:].reshape((-1,) + both_y.shape[2:])
    grad_w_outer = jnp.concatenate([share_of(outer_x, width), share_of(outer_z, width)], axis=0)
    return (
        loss_out.reshape(1),
        pooled[None],
        grad_tokens.reshape(rows_here, length, width),
        share_of(attn_x[0], width),
        b_query,
        share_of(attn_y[:tiles], width),
        share_of(attn_y[tiles:], width),
        b_value,
        share_of(attn_x[1], width),
        b_output,
        gain_attn,
        shift_attn,
        share_of(inner_sums, widening_offset.shape[0]),
        vector_sums[8 * rows :],
        grad_w_outer,
        b_outer,
        gain_ffn,
        shift_ffn,
    )


def solution(mesh):
    return jax.shard_map(
        body,
        mesh=mesh,
        in_specs=(
            P(("gx", "gy"), None, None),
            P(("gx", "gy"), None),
            P(("gx", "gy")),
            P(),
            P(),
            P(),
            P(),
            P(),
            P(),
            P(),
            P(),
            P(),
            P(),
            P(),
            P(),
            P(),
            P(),
            P(),
            P(),
        ),
        out_specs=(
            P(),
            P(("gx", "gy"), None, None),
            P(("gx", "gy"), None, None),
            P("gy", None),
            P("gy"),
            P("gy", None),
            P("gy", None),
            P("gy"),
            P("gy", None),
            P("gy"),
            P("gy"),
            P("gy"),
            P("gy", None),
            P("gy"),
            P("gy", None),
            P("gy"),
            P("gy"),
            P("gy"),
        ),
        check_vma=False,
    )
```

time: 692 us -> 231 us (0.33); the launches traced: 684 us -> 230 us
  waiting for transfers between devices: 338 us -> 63.5 us
  matrix products: 110 us -> 0 us
  Pallas kernels: 0 us -> 100 us
  blocking collectives: 96.4 us -> 0 us
  local copies, waits for them, and re-layouts: 94.7 us -> 14 us
  starting transfers between devices: 0.08 us -> 39 us
  between operations: 18 us -> 1.84 us
  other arithmetic: 27.2 us -> 11.2 us
    unnamed x4 -> x0, waiting for transfers between devices: 338 us -> none
    dot_general x29 -> x0, matrix products: 110 us -> none  [the longest x7 22.5 us: contract_rows(): lax.dot_general(left, right, (((0,), (0,)), ((), ())), preferred_element_...]
    pallas_call x0 -> x8, Pallas kernels: none -> 100 us  [the longest x1 34.4 us: forward_step(): pl.pallas_call(functools.partial(forward_kernel, segments, masks_x, masks...]
    ppermute x0 -> x32, waiting for transfers between devices: none -> 63.5 us  [swap_with(): return lax.ppermute(value, axis, [(i, i ^ bit) for i in range(count)])]
    all_gather x2 -> x0, blocking collectives: 56.8 us -> none  [the longest x1 44.3 us: body(): lax.all_gather(passage_directions, ('gx', 'gy'), axis=0, tiled=True)]
    concatenate x11 -> x3, local copies, waits for them, and re-layouts: 56.3 us -> 0.16 us  [the longest x1 0.08 us: body(): keep = jnp.concatenate([inner_keep, attn_keep_y], axis=1)]
    unnamed x1 -> x0, blocking collectives: 39.5 us -> none
    ppermute x0 -> x32, starting transfers between devices: none -> 39 us  [swap_with(): return lax.ppermute(value, axis, [(i, i ^ bit) for i in range(count)])]
  transfers between devices with their start and end apart: 2 -> 32, of which waited for: 2 -> 15; matrix products, arithmetic and copies ran while one was open for 2% -> 8% of each run, Pallas kernels for 0% -> 26%
where the time goes in v1:
time: 231 us; the launch traced here: 230 us
  Pallas kernels  100 us (43%)
  waiting for transfers between devices  63.5 us (27%)
  starting transfers between devices  39 us (17%)
  local copies, waits for them, and re-layouts  14 us (6%)
  other arithmetic  11.2 us (5%)
    ppermute x32, waiting for transfers between devices, swap_with(): return lax.ppermute(value, axis, [(i, i ^ bit) for i in range(count)])  63.5 us
    ppermute x32, starting transfers between devices, swap_with(): return lax.ppermute(value, axis, [(i, i ^ bit) for i in range(count)])  39 us
    pallas_call x1, Pallas kernels, forward_step(): pl.pallas_call(functools.partial(forward_kernel, segments, masks_x, masks...  34.4 us
    pallas_call x1, Pallas kernels, inner_step(): pl.pallas_call(functools.partial(inner_kernel, at), grid_spec=pltpu.Prefe...  15.3 us
    pallas_call x1, Pallas kernels, attend_back_step(): pl.pallas_call(functools.partial(attend_back_kernel, sizes.shape[1]), gri...  12.9 us
    pallas_call x1, Pallas kernels, outer_step(): pl.pallas_call(outer_kernel, grid=(width // wide,), in_specs=[any_spec(),...  9.25 us
    pallas_call x1, Pallas kernels, before_step(): pl.pallas_call(before_kernel, grid=(hidden_units // tile,), in_specs=[pl....  8.39 us
    pallas_call x1, Pallas kernels, attention_step(): pl.pallas_call(functools.partial(attention_kernel, token_at, attn_at), gr...  7.94 us
  transfers between devices with their start and end apart: 32, of which 15 were waited for; matrix products, arithmetic and copies ran while one was open for 8% of the time, Pallas kernels for 26%

profile of v1, /device:TPU:0, one launch (start us, length us, event | category | flops | bytes accessed | tf_op | source)
XLA Modules:
  0.0 229.8 jit_solution(16708299238658450610)
XLA Ops:
  0.7 34.4 %forward_step.1 = (bf16[512,768]{1,0:T(8,128)(2,1)}, bf16[512,768]{1,0:T(8,128)(2,1)}, bf16[768,512]{1,0:T(8,128)(2,1)}, bf16[512,768]{1,0:T(8,128)(2,1)}, f32[1...) custom-call(s32[1]{0:T(128)} %bitcast.1.here_ref, ...), custom_call_target="tpu_custom_call" | custom-call | flops 30799998976 | bytes 1000000 | tf_op jit(solution)/shard_map/forward_step/pallas_call | solution.py:453
  35.6 3.7 %collective-permute-start = (bf16[1,8,896]{2,1,0:T(8,128)(2,1)}, bf16[1,8,896]{2,1,0:T(8,128)(2,1)S(1)}, u32[]{:S(2)}, u32[]{:S(2)}) collective-permute-start(bf16[1,8,896]{2,1,0:T(8,128)(2,1)} %bitcast.99), channel_id=1, source_target_pairs={{0,8},{1,9},{2,10},{3,11},{4,12},{5,13},{6,14},{7,15},{8,0},{9,1},... | collective-permute-start | bytes 43016 | tf_op jit(solution)/shard_map/ppermute | solution.py:55
  39.3 1.9 collective-permute-done
  41.2 0.7 pad_maximum_fusion.7
  41.9 1.9 collective-permute-start.1
  43.8 2.0 collective-permute-done.1
  45.8 0.7 pad_maximum_fusion.6
  46.5 1.9 collective-permute-start.2
  48.4 2.3 %collective-permute-done.2 = bf16[4,8,896]{2,1,0:T(8,128)(2,1)S(1)} collective-permute-done((bf16[4,8,896]{2,1,0:T(8,128)(2,1)S(1)}, bf16[4,8,896]{2,1,0:T(8,128)(2,1)S(1)}, u32[]{:S(2)}, u32[]{:S(2)}) %collective-permute-start.2) | collective-permute-done | bytes 57376 | tf_op jit(solution)/shard_map/ppermute | solution.py:55
  50.7 0.7 pad_maximum_fusion.5
  51.5 1.9 collective-permute-start.4
  53.4 3.0 %collective-permute-done.4 = bf16[8,8,896]{2,1,0:T(8,128)(2,1)S(1)} collective-permute-done((bf16[8,8,896]{2,1,0:T(8,128)(2,1)S(1)}, bf16[8,8,896]{2,1,0:T(8,128)(2,1)S(1)}, u32[]{:S(2)}, u32[]{:S(2)}) %collective-permute-start.4) | collective-permute-done | bytes 114720 | tf_op jit(solution)/shard_map/ppermute | solution.py:55
  57.1 0.8 collective-permute-done.5
  57.9 0.8 pad_maximum_fusion.1.gathered_hbm
  58.8 5.5 %loss_step.1 = (f32[1,1]{1,0:T(1,128)}, f32[512,768]{1,0:T(8,128)}, bf16[512,768]{1,0:T(8,128)(2,1)}, f32[3,768]{1,0:T(4,128)}) custom-call(s32[1]{0:T(128)} %bitcast.place_ref, s32[1,8]{1,0:T(1,128)} %sizes_ref.5, f32[1]{0:T(128)S(6)} %copy.72.sharpness_ref, s32[1,128]{1,0:T(1,128)} %constant.23.clone.numbers_ref, ...), custom_call_target="tpu_custom_call" | custom-call | flops 4400000000 | bytes 1000000 | tf_op jit(solution)/shard_map/loss_step/pallas_call | solution.py:600
  64.5 8.4 %before_step.1 = (bf16[512,3072]{1,0:T(8,128)(2,1)}, f32[1,3072]{1,0:T(1,128)}) custom-call(bf16[512,768]{1,0:T(8,128)(2,1)} %get-tuple-element.81.branch_ref.branch_own_ref, bf16[512,3072]{1,0:T(8,128)(2,1)} %get-tuple-element.82.slope_ref, bf16[3072,768]{1,0:T(8,128)(2,1)} %narrowing_ref.1), custom_call_target="tpu_custom_call" | custom-call | flops 6600000000 | bytes 1000000 | tf_op jit(solution)/shard_map/before_step/pallas_call | solution.py:642
  72.9 0.9 copy-done.12
  74.2 0.6 reshape.130.lse_ref
  74.8 9.3 %outer_step.1 = (bf16[4,12,48,128]{3,2,1,0:T(8,128)(2,1)}, bf16[4,12,48,128]{3,2,1,0:T(8,128)(2,1)}, bf16[4,12,48,128]{3,2,1,0:T(8,128)(2,1)}, bf16[4,12,48,128]{3,2,1,0:T(8,128)(2,1)}) custom-call(bf16[8,336,512]{2,1,0:T(8,128)(2,1)} %get-tuple-element.85.own_ref, bf16[8,336,512]{2,1,0:T(8,128)(2,1)} %copy-done.11, ...), custom_call_target="tpu_custom_call" | custom-call | flops 6600000000 | bytes 1000000 | tf_op jit(solution)/shard_map/outer_step/pallas_call | solution.py:738
  84.1 1.7 copy-done.10
  85.8 1.8 collective-permute-start.8
  87.6 1.6 collective-permute-start.9
  89.2 15.3 %inner_step.1 = (bf16[8,12,48,128]{3,2,1,0:T(8,128)(2,1)}, bf16[8,12,48,128]{3,2,1,0:T(8,128)(2,1)}, f32[512,768]{1,0:T(8,128)}, bf16[512,768]{1,0:T(8,128)(2,1)...) custom-call(s32[1]{0:T(128)} %bitcast.6.side_ref, bf16[8,336,512]{2,1,0:T(8,128)(2,1)} %get-tuple-element.85.own_ref, ...), custom_call_target="tpu_custom_call" | custom-call | flops 13200000000 | bytes 1000000 | tf_op jit(solution)/shard_map/inner_step/pallas_call | solution.py:862
  104.6 12.9 %attend_back_step.1 = (bf16[3,512,768]{2,1,0:T(8,128)(2,1)}, f32[2,768]{1,0:T(2,128)}) custom-call(s32[1,8]{1,0:T(1,128)} %sizes_ref.5, bf16[512,768]{1,0:T(8,128)(2,1)} %get-tuple-element.99.query_ref, bf16[512,768]{1,0:T(8,128)(2,1)} %get-tuple-element.100.key_ref, bf16[768,512]{1,0:T(8,128)(2,1)} %get-tuple-element.101.key_t_ref, ...), custom_call_target="tpu_custom_call" | custom-call | flops 13200000000 | bytes 1000000 | tf_op jit(solution)/shard_map/attend_back_step/pallas_call | solution.py:986
  118.6 0.7 reduce.3
  119.5 2.7 %collective-permute-start.13 = (bf16[2,12,48,128]{3,2,1,0:T(8,128)(2,1)S(1)}, bf16[2,12,48,128]{3,2,1,0:T(8,128)(2,1)}, u32[]{:S(2)}, u32[]{:S(2)}) collective-permute-start(bf16[2,12,48,128]{3,2,1,0:T(8,128)(2,1)S(1)} %get-tuple-element.137), channel_id=1, source_target_pairs={{0,8},{1,9},{2,10},{3,11},{4,12},{5,13},{6,14},{7,15},{8,0},{9,1},... | collective-permute-start | bytes 884744 | tf_op jit(solution)/shard_map/ppermute | solution.py:55
  122.2 0.8 convert_add_fusion.3
  123.4 1.5 collective-permute-start.23
  125.0 6.5 %token_step.1 = f32[512,768]{1,0:T(8,128)} custom-call(f32[512,768]{1,0:T(8,128)} %get-tuple-element.107.hidden_ref, bf16[3,512,768]{2,1,0:T(8,128)(2,1)} %get-tuple-element.106.grads_ref.grads_own_ref, bf16[768,768]{1,0:T(8,128)(2,1)} %question_ref.1, bf16[768,768]{1,0:T(8,128)(2,1)} %lookup_ref.1, bf16[768,768]{1,0:T(8,128)(2,1)} %content_ref.1), custom_call_target="tpu_custom_call" | custom-call | flops 5500000256 | bytes 1000000 | tf_op jit(solution)/shard_map/token_step/pallas_call | solution.py:1032
  131.5 7.9 %attention_step.1 = (bf16[4,2,6,48,128]{4,3,2,1,0:T(8,128)(2,1)}, bf16[4,2,6,48,128]{4,3,2,1,0:T(8,128)(2,1)}, bf16[8,6,48,128]{3,2,1,0:T(8,128)(2,1)}, bf16[8,6,48,128]{3,2,1,0:T(8,128)(2,1)}) custom-call(s32[1]{0:T(128)} %bitcast.6.side_ref, bf16[8,336,512]{2,1,0:T(8,128)(2,1)} %get-tuple-element.85.own_ref, bf16[8,336,512]{2,1,0:T(8,128)(2,1)} %copy-done.11, ...), custom_call_target="tpu_custom_call" | custom-call | flops 5500000256 | bytes 1000000 | tf_op jit(solution)/shard_map/attention_step/pallas_call | solution.py:1099
  139.5 0.6 pad_maximum_fusion.8
  140.1 1.5 reshape.133
  141.6 1.5 copy.45
  143.1 1.5 reshape.134
  144.6 0.7 constant_dynamic-update-slice_fusion.1
  145.8 4.3 %collective-permute-done.18 = f32[8,576]{1,0:T(8,128)S(1)} collective-permute-done((f32[8,576]{1,0:T(8,128)S(1)}, f32[8,576]{1,0:T(8,128)S(1)}, u32[]{:S(2)}, u32[]{:S(2)}) %collective-permute-start.18) | collective-permute-done | bytes 18464 | tf_op jit(solution)/shard_map/ppermute | solution.py:55
  150.1 1.7 collective-permute-start.19
  151.9 2.0 collective-permute-done.19
  153.9 0.6 collective-permute-start.20
  154.5 0.9 fusion.4
  155.4 1.6 collective-permute-start.30
  157.7 0.9 fusion.7
  159.9 1.8 collective-permute-start.22
  161.8 13.1 %collective-permute-done.22 = f32[1,576]{1,0:T(1,128)S(1)} collective-permute-done((f32[1,576]{1,0:T(1,128)S(1)}, f32[1,576]{1,0:T(1,128)S(1)}, u32[]{:S(2)}, u32[]{:S(2)}) %collective-permute-start.22) | collective-permute-done | bytes 2336 | tf_op jit(solution)/shard_map/ppermute | solution.py:55
  175.4 0.6 slice_bitcast_fusion.2
  176.0 1.0 fusion.16
  177.0 1.0 fusion.15
  179.1 1.5 collective-permute-start.25
  180.8 1.7 collective-permute-start.15
  182.5 3.6 %collective-permute-done.31 = bf16[24,48,128]{2,1,0:T(8,128)(2,1)S(1)} collective-permute-done((bf16[24,48,128]{2,1,0:T(8,128)(2,1)S(1)}, bf16[24,48,128]{2,1,0:T(8,128)(2,1)S(1)}, u32[]{:S(2)}, u32[]{:S(2)}) %collective-permute-start.31) | collective-permute-done | bytes 294944 | tf_op jit(solution)/shard_map/ppermute | solution.py:55
  186.6 1.7 collective-permute-done.15
  188.3 2.6 %collective-permute-start.16 = (bf16[1,2,6,48,128]{4,3,2,1,0:T(8,128)(2,1)S(1)}, bf16[1,2,6,48,128]{4,3,2,1,0:T(8,128)(2,1)S(1)}, u32[]{:S(2)}, u32[]{:S(2)}) collective-permute-start(bf16[1,2,6,48,128]{4,3,2,1,0:T(8,128)(2,1)S(1)} %fusion.10), channel_id=1, source_target_pairs={{0,8},{1,9},{2,10},{3,11},{4,12},{5,13},{6,14},{7,15},{8,0},{9,1},... | collective-permute-start | bytes 442376 | tf_op jit(solution)/shard_map/ppermute | solution.py:55
  190.9 8.9 %collective-permute-done.25 = bf16[4,18,48,128]{3,2,1,0:T(8,128)(2,1)S(1)} collective-permute-done((bf16[4,18,48,128]{3,2,1,0:T(8,128)(2,1)S(1)}, bf16[4,18,48,128]{3,2,1,0:T(8,128)(2,1)S(1)}, u32[]{:S(2)}, u32[]{:S(2)}) %collective-permute-start.25) | collective-permute-done | bytes 884768 | tf_op jit(solution)/shard_map/ppermute | solution.py:55
  200.0 1.4 collective-permute-start.26
  201.5 0.9 pad_maximum_fusion
  202.4 1.6 collective-permute-start.17
  204.0 6.3 %collective-permute-done.26 = bf16[2,18,48,128]{3,2,1,0:T(8,128)(2,1)S(1)} collective-permute-done((bf16[2,18,48,128]{3,2,1,0:T(8,128)(2,1)S(1)}, bf16[2,18,48,128]{3,2,1,0:T(8,128)(2,1)S(1)}, u32[]{:S(2)}, u32[]{:S(2)}) %collective-permute-start.26) | collective-permute-done | bytes 442400 | tf_op jit(solution)/shard_map/ppermute | solution.py:55
  210.4 2.3 %collective-permute-start.27 = (bf16[1,18,48,128]{3,2,1,0:T(8,128)(2,1)S(1)}, bf16[1,18,48,128]{3,2,1,0:T(8,128)(2,1)S(1)}, u32[]{:S(2)}, u32[]{:S(2)}) collective-permute-start(bf16[1,18,48,128]{3,2,1,0:T(8,128)(2,1)S(1)} %fusion.1), channel_id=1, source_target_pairs={{0,8},{1,9},{2,10},{3,11},{4,12},{5,13},{6,14},{7,15},{8,0},{9,1},... | collective-permute-start | bytes 663560 | tf_op jit(solution)/shard_map/ppermute | solution.py:55
  212.7 7.9 %collective-permute-done.27 = bf16[1,18,48,128]{3,2,1,0:T(8,128)(2,1)S(1)} collective-permute-done((bf16[1,18,48,128]{3,2,1,0:T(8,128)(2,1)S(1)}, bf16[1,18,48,128]{3,2,1,0:T(8,128)(2,1)S(1)}, u32[]{:S(2)}, u32[]{:S(2)}) %collective-permute-start.27) | collective-permute-done | bytes 221216 | tf_op jit(solution)/shard_map/ppermute | solution.py:55
  220.7 0.8 collective-permute-start.28
  221.6 5.2 %collective-permute-done.28 = bf16[18,48,128]{2,1,0:T(8,128)(2,1)S(1)} collective-permute-done((bf16[18,48,128]{2,1,0:T(8,128)(2,1)S(1)}, bf16[18,48,128]{2,1,0:T(8,128)(2,1)S(1)}, u32[]{:S(2)}, u32[]{:S(2)}) %collective-permute-start.28) | collective-permute-done | bytes 221216 | tf_op jit(solution)/shard_map/ppermute | solution.py:55
  227.3 0.9 copy.68
  228.2 0.8 copy_bitcast_fusion.3
  229.0 0.8 copy_bitcast_fusion.5
  (102 shorter events, 9.0 us)
Async XLA Ops:
  35.1 16.4 %collective-permute-start.3 = (bf16[8,336,512]{2,1,0:T(8,128)(2,1)}, bf16[8,336,512]{2,1,0:T(8,128)(2,1)S(1)}, u32[]{:S(2)}, u32[]{:S(2)}) collective-permute-start(bf16[8,336,512]{2,1,0:T(8,128)(2,1)} %get-tuple-element.75), channel_id=1, source_target_pairs={{0,1},{1,0},{2,3},{3,2},{4,5},{5,4},{6,7},{7,6},{8,9},{9,8},{10,11... | collective-permute-start | bytes 8257544 | tf_op jit(solution)/shard_map/ppermute | solution.py:55
  35.6 5.6 %collective-permute-start = (bf16[1,8,896]{2,1,0:T(8,128)(2,1)}, bf16[1,8,896]{2,1,0:T(8,128)(2,1)S(1)}, u32[]{:S(2)}, u32[]{:S(2)}) collective-permute-start(bf16[1,8,896]{2,1,0:T(8,128)(2,1)} %bitcast.99), channel_id=1, source_target_pairs={{0,8},{1,9},{2,10},{3,11},{4,12},{5,13},{6,14},{7,15},{8,0},{9,1},... | collective-permute-start | bytes 43016 | tf_op jit(solution)/shard_map/ppermute | solution.py:55
  41.9 3.9 %collective-permute-start.1 = (bf16[2,8,896]{2,1,0:T(8,128)(2,1)S(1)}, bf16[2,8,896]{2,1,0:T(8,128)(2,1)S(1)}, u32[]{:S(2)}, u32[]{:S(2)}) collective-permute-start(bf16[2,8,896]{2,1,0:T(8,128)(2,1)S(1)} %pad_maximum_fusion.7), channel_id=1, source_target_pairs={{0,4},{1,5},{2,6},{3,7},{4,0},{5,1},{6,2},{7,3},{8,12},{9,13},{10,... | collective-permute-start | bytes 86024 | tf_op jit(solution)/shard_map/ppermute | solution.py:55
  46.5 4.2 %collective-permute-start.2 = (bf16[4,8,896]{2,1,0:T(8,128)(2,1)S(1)}, bf16[4,8,896]{2,1,0:T(8,128)(2,1)S(1)}, u32[]{:S(2)}, u32[]{:S(2)}) collective-permute-start(bf16[4,8,896]{2,1,0:T(8,128)(2,1)S(1)} %pad_maximum_fusion.6), channel_id=1, source_target_pairs={{0,16},{16,0},{1,17},{17,1},{2,18},{18,2},{3,19},{19,3},{4,20},{20... | collective-permute-start | bytes 172040 | tf_op jit(solution)/shard_map/ppermute | solution.py:55
  51.5 1.9 copy-start.11
  51.5 4.9 %collective-permute-start.4 = (bf16[8,8,896]{2,1,0:T(8,128)(2,1)S(1)}, bf16[8,8,896]{2,1,0:T(8,128)(2,1)S(1)}, u32[]{:S(2)}, u32[]{:S(2)}) collective-permute-start(bf16[8,8,896]{2,1,0:T(8,128)(2,1)S(1)} %pad_maximum_fusion.5), channel_id=1, source_target_pairs={{0,2},{1,3},{2,0},{3,1},{4,6},{5,7},{6,4},{7,5},{8,10},{9,11},{10,... | collective-permute-start | bytes 344072 | tf_op jit(solution)/shard_map/ppermute | solution.py:55
  56.4 1.6 collective-permute-start.5
  64.3 8.6 %collective-permute-start.6 = (bf16[512,768]{1,0:T(8,128)(2,1)}, bf16[512,768]{1,0:T(8,128)(2,1)S(1)}, u32[]{:S(2)}, u32[]{:S(2)}) collective-permute-start(bf16[512,768]{1,0:T(8,128)(2,1)} %get-tuple-element.81.branch_ref.branch_own_ref), channel_id=1, source_target_pairs={{0,1},{1,0},{2,3},{3,2},{4,5},{5,4},{6,7},{7,6},{8,9},{9,8},{10,11... | collective-permute-start | bytes 2359304 | tf_op jit(solution)/shard_map/ppermute | solution.py:55
  64.5 9.7 %copy-start.5 = (f32[12,512]{1,0:T(8,128)S(1)}, f32[12,512]{1,0:T(8,128)}, u32[]{:S(2)}) copy-start(f32[12,512]{1,0:T(8,128)} %get-tuple-element.103) | copy-start | bytes 73732
  72.9 0.9 copy-start.12
  73.8 10.3 %collective-permute-start.7 = (bf16[512,3072]{1,0:T(8,128)(2,1)}, bf16[512,3072]{1,0:T(8,128)(2,1)S(1)}, u32[]{:S(2)}, u32[]{:S(2)}) collective-permute-start(bf16[512,3072]{1,0:T(8,128)(2,1)} %get-tuple-element.84.grad_own_ref), channel_id=1, source_target_pairs={{0,1},{1,0},{2,3},{3,2},{4,5},{5,4},{6,7},{7,6},{8,9},{9,8},{10,11... | collective-permute-start | bytes 9437192 | tf_op jit(solution)/shard_map/ppermute | solution.py:55
  84.1 1.7 copy-start.10
  85.8 18.7 %collective-permute-start.8 = (bf16[4,12,48,128]{3,2,1,0:T(8,128)(2,1)}, bf16[4,12,48,128]{3,2,1,0:T(8,128)(2,1)S(1)}, u32[]{:S(2)}, u32[]{:S(2)}) collective-permute-start(bf16[4,12,48,128]{3,2,1,0:T(8,128)(2,1)} %get-tuple-element.90), channel_id=1, source_target_pairs={{0,2},{1,3},{2,0},{3,1},{4,6},{5,7},{6,4},{7,5},{8,10},{9,11},{10,... | collective-permute-start | bytes 1769480 | tf_op jit(solution)/shard_map/ppermute | solution.py:55
  87.6 16.9 %collective-permute-start.9 = (bf16[4,12,48,128]{3,2,1,0:T(8,128)(2,1)}, bf16[4,12,48,128]{3,2,1,0:T(8,128)(2,1)S(1)}, u32[]{:S(2)}, u32[]{:S(2)}) collective-permute-start(bf16[4,12,48,128]{3,2,1,0:T(8,128)(2,1)} %get-tuple-element.91), channel_id=1, source_target_pairs={{0,4},{1,5},{2,6},{3,7},{4,0},{5,1},{6,2},{7,3},{8,12},{9,13},{10,... | collective-permute-start | bytes 1769480 | tf_op jit(solution)/shard_map/ppermute | solution.py:55
  104.5 13.0 %collective-permute-start.10 = (bf16[512,768]{1,0:T(8,128)(2,1)}, bf16[512,768]{1,0:T(8,128)(2,1)}, u32[]{:S(2)}, u32[]{:S(2)}) collective-permute-start(bf16[512,768]{1,0:T(8,128)(2,1)} %get-tuple-element.98.branch_own_ref), channel_id=1, source_target_pairs={{0,1},{1,0},{2,3},{3,2},{4,5},{5,4},{6,7},{7,6},{8,9},{9,8},{10,11... | collective-permute-start | bytes 2359304 | tf_op jit(solution)/shard_map/ppermute | solution.py:55
  104.6 14.0 %copy-start.8 = (f32[1,3072]{1,0:T(1,128)S(1)}, f32[1,3072]{1,0:T(1,128)}, u32[]{:S(2)}) copy-start(f32[1,3072]{1,0:T(1,128)} %get-tuple-element.123) | copy-start | bytes 36868
  104.6 14.8 %copy-start.4 = (bf16[4,12,48,128]{3,2,1,0:T(8,128)(2,1)S(1)}, bf16[4,12,48,128]{3,2,1,0:T(8,128)(2,1)}, u32[]{:S(2)}) copy-start(bf16[4,12,48,128]{3,2,1,0:T(8,128)(2,1)} %get-tuple-element.114) | copy-start | bytes 1769476
  117.5 4.7 %copy-start.3 = (bf16[4,12,48,128]{3,2,1,0:T(8,128)(2,1)S(1)}, bf16[4,12,48,128]{3,2,1,0:T(8,128)(2,1)}, u32[]{:S(2)}) copy-start(bf16[4,12,48,128]{3,2,1,0:T(8,128)(2,1)} %get-tuple-element.112) | copy-start | bytes 1769476
  117.5 14.0 %collective-permute-start.11 = (bf16[3,512,768]{2,1,0:T(8,128)(2,1)}, bf16[3,512,768]{2,1,0:T(8,128)(2,1)}, u32[]{:S(2)}, u32[]{:S(2)}) collective-permute-start(bf16[3,512,768]{2,1,0:T(8,128)(2,1)} %get-tuple-element.106.grads_ref.grads_own_ref), channel_id=1, source_target_pairs={{0,1},{1,0},{2,3},{3,2},{4,5},{5,4},{6,7},{7,6},{8,9},{9,8},{10,11... | collective-permute-start | bytes 7077896 | tf_op jit(solution)/shard_map/ppermute | solution.py:55
  119.5 20.0 %collective-permute-start.13 = (bf16[2,12,48,128]{3,2,1,0:T(8,128)(2,1)S(1)}, bf16[2,12,48,128]{3,2,1,0:T(8,128)(2,1)}, u32[]{:S(2)}, u32[]{:S(2)}) collective-permute-start(bf16[2,12,48,128]{3,2,1,0:T(8,128)(2,1)S(1)} %get-tuple-element.137), channel_id=1, source_target_pairs={{0,8},{1,9},{2,10},{3,11},{4,12},{5,13},{6,14},{7,15},{8,0},{9,1},... | collective-permute-start | bytes 884744 | tf_op jit(solution)/shard_map/ppermute | solution.py:55
  123.0 16.4 %collective-permute-start.12 = (bf16[2,12,48,128]{3,2,1,0:T(8,128)(2,1)}, bf16[2,12,48,128]{3,2,1,0:T(8,128)(2,1)}, u32[]{:S(2)}, u32[]{:S(2)}) collective-permute-start(bf16[2,12,48,128]{3,2,1,0:T(8,128)(2,1)} %get-tuple-element.135), channel_id=1, source_target_pairs={{0,4},{1,5},{2,6},{3,7},{4,0},{5,1},{6,2},{7,3},{8,12},{9,13},{10,... | collective-permute-start | bytes 884744 | tf_op jit(solution)/shard_map/ppermute | solution.py:55
  123.4 28.4 %collective-permute-start.23 = (bf16[8,12,48,128]{3,2,1,0:T(8,128)(2,1)}, bf16[8,12,48,128]{3,2,1,0:T(8,128)(2,1)S(1)}, u32[]{:S(2)}, u32[]{:S(2)}) collective-permute-start(bf16[8,12,48,128]{3,2,1,0:T(8,128)(2,1)} %get-tuple-element.126), channel_id=1, source_target_pairs={{0,16},{16,0},{1,17},{17,1},{2,18},{18,2},{3,19},{19,3},{4,20},{20... | collective-permute-start | bytes 3538952 | tf_op jit(solution)/shard_map/ppermute | solution.py:55
  131.5 8.0 %copy-start.6 = (f32[3,768]{1,0:T(4,128)S(1)}, f32[3,768]{1,0:T(4,128)}, u32[]{:S(2)}) copy-start(f32[3,768]{1,0:T(4,128)} %get-tuple-element.122) | copy-start | bytes 27652
  131.5 8.0 %copy-start.7 = (f32[3,768]{1,0:T(4,128)S(1)}, f32[3,768]{1,0:T(4,128)}, u32[]{:S(2)}) copy-start(f32[3,768]{1,0:T(4,128)} %get-tuple-element.121) | copy-start | bytes 27652
  131.5 8.0 %copy-start.9 = (f32[2,768]{1,0:T(2,128)S(1)}, f32[2,768]{1,0:T(2,128)}, u32[]{:S(2)}) copy-start(f32[2,768]{1,0:T(2,128)} %get-tuple-element.120) | copy-start | bytes 18436
  131.5 14.3 %copy-start = (bf16[8,12,48,128]{3,2,1,0:T(8,128)(2,1)S(1)}, bf16[8,12,48,128]{3,2,1,0:T(8,128)(2,1)}, u32[]{:S(2)}) copy-start(bf16[8,12,48,128]{3,2,1,0:T(8,128)(2,1)} %get-tuple-element.124) | copy-start | bytes 3538948
  145.3 4.7 %collective-permute-start.18 = (f32[8,576]{1,0:T(8,128)S(1)}, f32[8,576]{1,0:T(8,128)S(1)}, u32[]{:S(2)}, u32[]{:S(2)}) collective-permute-start(f32[8,576]{1,0:T(8,128)S(1)} %slice_select_fusion), channel_id=1, source_target_pairs={{0,8},{1,9},{2,10},{3,11},{4,12},{5,13},{6,14},{7,15},{8,0},{9,1},... | collective-permute-start | bytes 55304 | tf_op jit(solution)/shard_map/ppermute | solution.py:55
  150.1 8.9 %copy-start.13 = (bf16[4,2,6,48,128]{4,3,2,1,0:T(8,128)(2,1)S(1)}, bf16[4,2,6,48,128]{4,3,2,1,0:T(8,128)(2,1)}, u32[]{:S(2)}) copy-start(bf16[4,2,6,48,128]{4,3,2,1,0:T(8,128)(2,1)} %get-tuple-element.119) | copy-start | bytes 1769476
  150.1 9.5 %copy-start.14 = (bf16[8,6,48,128]{3,2,1,0:T(8,128)(2,1)S(1)}, bf16[8,6,48,128]{3,2,1,0:T(8,128)(2,1)}, u32[]{:S(2)}) copy-start(bf16[8,6,48,128]{3,2,1,0:T(8,128)(2,1)} %get-tuple-element.127) | copy-start | bytes 1769476
  150.1 11.6 %copy-start.1 = (bf16[8,6,48,128]{3,2,1,0:T(8,128)(2,1)S(1)}, bf16[8,6,48,128]{3,2,1,0:T(8,128)(2,1)}, u32[]{:S(2)}) copy-start(bf16[8,6,48,128]{3,2,1,0:T(8,128)(2,1)} %get-tuple-element.125) | copy-start | bytes 1769476
  150.1 3.7 %collective-permute-start.19 = (f32[4,576]{1,0:T(4,128)S(1)}, f32[4,576]{1,0:T(4,128)S(1)}, u32[]{:S(2)}, u32[]{:S(2)}) collective-permute-start(f32[4,576]{1,0:T(4,128)S(1)} %slice_select_fusion.1), channel_id=1, source_target_pairs={{0,4},{1,5},{2,6},{3,7},{4,0},{5,1},{6,2},{7,3},{8,12},{9,13},{10,... | collective-permute-start | bytes 27656 | tf_op jit(solution)/shard_map/ppermute | solution.py:55
  153.9 3.7 %collective-permute-start.20 = (f32[2,576]{1,0:T(2,128)S(1)}, f32[2,576]{1,0:T(2,128)S(1)}, u32[]{:S(2)}, u32[]{:S(2)}) collective-permute-start(f32[2,576]{1,0:T(2,128)S(1)} %broadcast_select_fusion.2), channel_id=1, source_target_pairs={{0,2},{1,3},{2,0},{3,1},{4,6},{5,7},{6,4},{7,5},{8,10},{9,11},{10,... | collective-permute-start | bytes 13832 | tf_op jit(solution)/shard_map/ppermute | solution.py:55
  155.4 20.6 %collective-permute-start.30 = (bf16[1,12,48,128]{3,2,1,0:T(8,128)(2,1)S(1)}, bf16[1,12,48,128]{3,2,1,0:T(8,128)(2,1)S(1)}, u32[]{:S(2)}, u32[]{:S(2)}) collective-permute-start(bf16[1,12,48,128]{3,2,1,0:T(8,128)(2,1)S(1)} %fusion.4), channel_id=1, source_target_pairs={{0,2},{1,3},{2,0},{3,1},{4,6},{5,7},{6,4},{7,5},{8,10},{9,11},{10,... | collective-permute-start | bytes 442376 | tf_op jit(solution)/shard_map/ppermute | solution.py:55
  157.6 2.3 collective-permute-start.21
  158.6 18.4 %collective-permute-start.29 = (bf16[1,12,48,128]{3,2,1,0:T(8,128)(2,1)S(1)}, bf16[1,12,48,128]{3,2,1,0:T(8,128)(2,1)S(1)}, u32[]{:S(2)}, u32[]{:S(2)}) collective-permute-start(bf16[1,12,48,128]{3,2,1,0:T(8,128)(2,1)S(1)} %fusion.7), channel_id=1, source_target_pairs={{0,8},{1,9},{2,10},{3,11},{4,12},{5,13},{6,14},{7,15},{8,0},{9,1},... | collective-permute-start | bytes 442376 | tf_op jit(solution)/shard_map/ppermute | solution.py:55
  159.0 21.6 %collective-permute-start.14 = (bf16[4,2,6,48,128]{4,3,2,1,0:T(8,128)(2,1)S(1)}, bf16[4,2,6,48,128]{4,3,2,1,0:T(8,128)(2,1)S(1)}, u32[]{:S(2)}, u32[]{:S(2)}) collective-permute-start(bf16[4,2,6,48,128]{4,3,2,1,0:T(8,128)(2,1)S(1)} %copy-done.13), channel_id=1, source_target_pairs={{0,2},{1,3},{2,0},{3,1},{4,6},{5,7},{6,4},{7,5},{8,10},{9,11},{10,... | collective-permute-start | bytes 1769480 | tf_op jit(solution)/shard_map/ppermute | solution.py:55
  159.6 19.0 %collective-permute-start.24 = (bf16[8,6,48,128]{3,2,1,0:T(8,128)(2,1)S(1)}, bf16[8,6,48,128]{3,2,1,0:T(8,128)(2,1)S(1)}, u32[]{:S(2)}, u32[]{:S(2)}) collective-permute-start(bf16[8,6,48,128]{3,2,1,0:T(8,128)(2,1)S(1)} %copy-done.14), channel_id=1, source_target_pairs={{0,16},{16,0},{1,17},{17,1},{2,18},{18,2},{3,19},{19,3},{4,20},{20... | collective-permute-start | bytes 1769480 | tf_op jit(solution)/shard_map/ppermute | solution.py:55
  159.9 15.0 %collective-permute-start.22 = (f32[1,576]{1,0:T(1,128)S(1)}, f32[1,576]{1,0:T(1,128)S(1)}, u32[]{:S(2)}, u32[]{:S(2)}) collective-permute-start(f32[1,576]{1,0:T(1,128)S(1)} %fusion.17), channel_id=1, source_target_pairs={{0,16},{16,0},{1,17},{17,1},{2,18},{18,2},{3,19},{19,3},{4,20},{20... | collective-permute-start | bytes 6920 | tf_op jit(solution)/shard_map/ppermute | solution.py:55
  178.0 8.1 %collective-permute-start.31 = (bf16[24,48,128]{2,1,0:T(8,128)(2,1)S(1)}, bf16[24,48,128]{2,1,0:T(8,128)(2,1)S(1)}, u32[]{:S(2)}, u32[]{:S(2)}) collective-permute-start(bf16[24,48,128]{2,1,0:T(8,128)(2,1)S(1)} %pad_maximum_fusion.3), channel_id=1, source_target_pairs={{0,16},{16,0},{1,17},{17,1},{2,18},{18,2},{3,19},{19,3},{4,20},{20... | collective-permute-start | bytes 884744 | tf_op jit(solution)/shard_map/ppermute | solution.py:55
  178.7 2.0 copy-start.2
  179.1 20.7 %collective-permute-start.25 = (bf16[4,18,48,128]{3,2,1,0:T(8,128)(2,1)S(1)}, bf16[4,18,48,128]{3,2,1,0:T(8,128)(2,1)S(1)}, u32[]{:S(2)}, u32[]{:S(2)}) collective-permute-start(bf16[4,18,48,128]{3,2,1,0:T(8,128)(2,1)S(1)} %get-tuple-element.130), channel_id=1, source_target_pairs={{0,2},{1,3},{2,0},{3,1},{4,6},{5,7},{6,4},{7,5},{8,10},{9,11},{10,... | collective-permute-start | bytes 2654216 | tf_op jit(solution)/shard_map/ppermute | solution.py:55
  180.8 7.5 %collective-permute-start.15 = (bf16[2,2,6,48,128]{4,3,2,1,0:T(8,128)(2,1)S(1)}, bf16[2,2,6,48,128]{4,3,2,1,0:T(8,128)(2,1)S(1)}, u32[]{:S(2)}, u32[]{:S(2)}) collective-permute-start(bf16[2,2,6,48,128]{4,3,2,1,0:T(8,128)(2,1)S(1)} %get-tuple-element.138), channel_id=1, source_target_pairs={{0,4},{1,5},{2,6},{3,7},{4,0},{5,1},{6,2},{7,3},{8,12},{9,13},{10,... | collective-permute-start | bytes 884744 | tf_op jit(solution)/shard_map/ppermute | solution.py:55
  188.3 14.0 %collective-permute-start.16 = (bf16[1,2,6,48,128]{4,3,2,1,0:T(8,128)(2,1)S(1)}, bf16[1,2,6,48,128]{4,3,2,1,0:T(8,128)(2,1)S(1)}, u32[]{:S(2)}, u32[]{:S(2)}) collective-permute-start(bf16[1,2,6,48,128]{4,3,2,1,0:T(8,128)(2,1)S(1)} %fusion.10), channel_id=1, source_target_pairs={{0,8},{1,9},{2,10},{3,11},{4,12},{5,13},{6,14},{7,15},{8,0},{9,1},... | collective-permute-start | bytes 442376 | tf_op jit(solution)/shard_map/ppermute | solution.py:55
  200.0 10.3 %collective-permute-start.26 = (bf16[2,18,48,128]{3,2,1,0:T(8,128)(2,1)S(1)}, bf16[2,18,48,128]{3,2,1,0:T(8,128)(2,1)S(1)}, u32[]{:S(2)}, u32[]{:S(2)}) collective-permute-start(bf16[2,18,48,128]{3,2,1,0:T(8,128)(2,1)S(1)} %get-tuple-element.132), channel_id=1, source_target_pairs={{0,4},{1,5},{2,6},{3,7},{4,0},{5,1},{6,2},{7,3},{8,12},{9,13},{10,... | collective-permute-start | bytes 1327112 | tf_op jit(solution)/shard_map/ppermute | solution.py:55
  202.4 10.3 %collective-permute-start.17 = (bf16[2,6,48,128]{3,2,1,0:T(8,128)(2,1)S(1)}, bf16[2,6,48,128]{3,2,1,0:T(8,128)(2,1)S(1)}, u32[]{:S(2)}, u32[]{:S(2)}) collective-permute-start(bf16[2,6,48,128]{3,2,1,0:T(8,128)(2,1)S(1)} %fusion.14), channel_id=1, source_target_pairs={{0,16},{16,0},{1,17},{17,1},{2,18},{18,2},{3,19},{19,3},{4,20},{20... | collective-permute-start | bytes 442376 | tf_op jit(solution)/shard_map/ppermute | solution.py:55
  210.4 10.3 %collective-permute-start.27 = (bf16[1,18,48,128]{3,2,1,0:T(8,128)(2,1)S(1)}, bf16[1,18,48,128]{3,2,1,0:T(8,128)(2,1)S(1)}, u32[]{:S(2)}, u32[]{:S(2)}) collective-permute-start(bf16[1,18,48,128]{3,2,1,0:T(8,128)(2,1)S(1)} %fusion.1), channel_id=1, source_target_pairs={{0,8},{1,9},{2,10},{3,11},{4,12},{5,13},{6,14},{7,15},{8,0},{9,1},... | collective-permute-start | bytes 663560 | tf_op jit(solution)/shard_map/ppermute | solution.py:55
  220.7 6.1 %collective-permute-start.28 = (bf16[18,48,128]{2,1,0:T(8,128)(2,1)S(1)}, bf16[18,48,128]{2,1,0:T(8,128)(2,1)S(1)}, u32[]{:S(2)}, u32[]{:S(2)}) collective-permute-start(bf16[18,48,128]{2,1,0:T(8,128)(2,1)S(1)} %fusion.13), channel_id=1, source_target_pairs={{0,16},{16,0},{1,17},{17,1},{2,18},{18,2},{3,19},{19,3},{4,20},{20... | collective-permute-start | bytes 663560 | tf_op jit(solution)/shard_map/ppermute | solution.py:55
